TPU v7x, 32 devices: a whole 2x2x4 slice. The times are simulated.
32 devices in a mesh: runs: 2 (over x), gx: 16 (over z, y, core).
Axes of the slice: x: 2, y: 2, z: 4, core: 2. Of those that a mesh axis runs over, the one named last changes fastest.
Arguments:
- frac: float32 [3, 524288], P(None, ('runs', 'gx')), parts along dimension 1, may hold values from 0 to 1
- velocity: float32 [3, 524288], P(None, ('runs', 'gx')), parts along dimension 1, may hold values from -6 to 6
- mass: float32 [524288], P(('runs', 'gx')), parts along dimension 0, may hold values from 0.5 to 2
- particle_cell: int32 [524288], P(('runs', 'gx')), parts along dimension 0, may hold values from 0 to 8191, as said below
- tile_count: int32 [32], P(('runs', 'gx')), parts along dimension 0, may hold values from 2048 to 16384, as said below
- time_step: float32 [2], P('runs'), parts along dimension 0, may hold values from 0.1 to 0.2
Outputs:
- new_frac: float32 [3, 524288], P(None, ('runs', 'gx')), parts along dimension 1
- new_velocity: float32 [3, 524288], P(None, ('runs', 'gx')), parts along dimension 1
- next_step: float32 [2], P('runs'), parts along dimension 0
There are 2 independent parts, one for each index of `runs`. A program takes and returns all parts, laid end to end along the dimension named above; each array names one. Nothing has to cross between parts.
Inputs may be any that keep to these rules, and one draw needn't show every extreme that they name: `particle_cell`: within each tile the slots' cell numbers never fall; live slots come first and lie in cells with z <= 126; empty slots name the tile's last cell. `tile_count`: some tile is full in every run.
All inputs are finite; a program needn't handle non-finite values.
Results may differ from a plain program's by a relative error of at most 0.0003.
Values sent between devices are 32-bit elements; how exact they have to be, the bound alone decides.
No kernel may reach another device: no remote copies, remote signals or barrier semaphores. Data moves between devices by JAX's collectives and lax.ppermute only.
A program may use at most 64 MiB of HBM per device.

v0:
```python
import jax
import jax.numpy as jnp
from jax import lax
from jax.sharding import PartitionSpec as P

CX = 2
NY = 32
NZ = 128
PBLOCK = 2048


mass_floor = 0.25
stiffness = 2.0
press_floor = 1.0
grain_size = 0.5
inertia_ref = 0.3
mu_static = 0.38
mu_limit = 0.64
rate_floor = 0.5
gravity_x = 0.5
gravity_z = -0.866
flip_share = 0.95
courant = 0.4
wave_speed = 2.0
components = ((0, 3, 4), (3, 1, 5), (4, 5, 2))
highest = lax.Precision.HIGHEST


def shifted(array, axis, by):
    devices = lax.axis_size(axis)
    return lax.ppermute(array, axis, [(i, (i + by) % devices) for i in range(devices)])


def pair_up(field, axis):
    return field + jnp.roll(field, -1, axis)


def step_up(field, axis):
    return jnp.roll(field, -1, axis) - field


def pair_down(field, axis):
    return field + jnp.roll(field, 1, axis)


def step_down(field, axis):
    return field - jnp.roll(field, 1, axis)


def cell_gradient(extended, direction):
    if direction == 0:
        grad = pair_up(pair_up(extended[1:] - extended[:-1], 1), 2)
    elif direction == 1:
        grad = pair_up(step_up(extended[1:] + extended[:-1], 1), 2)
    else:
        grad = step_up(pair_up(extended[1:] + extended[:-1], 1), 2)
    return 0.25 * grad


def node_divergence(layers, direction):
    if direction == 0:
        summed = pair_down(pair_down(layers, 1), 2)
        result = summed[1:] - summed[:-1]
    elif direction == 1:
        result = step_down(pair_down(layers[1:] + layers[:-1], 2), 1)
    else:
        result = step_down(pair_down(layers[1:] + layers[:-1], 1), 2)
    return 0.25 * result


def node_forces(layers):
    return jnp.stack(
        [
            node_divergence(layers[components[a][0]], 0)
            + node_divergence(layers[components[a][1]], 1)
            + node_divergence(layers[components[a][2]], 2)
            for a in range(3)
        ]
    )


def stresses(grads, density, keep):
    dxx = grads[0][0]
    dyy = grads[1][1]
    dzz = grads[2][2]
    dxy = 0.5 * (grads[0][1] + grads[1][0])
    dxz = 0.5 * (grads[0][2] + grads[2][0])
    dyz = 0.5 * (grads[1][2] + grads[2][1])
    second = dxx * dxx + dyy * dyy + dzz * dzz + 2.0 * (dxy * dxy + dxz * dxz + dyz * dyz)
    rate = jnp.sqrt(2.0 * second + rate_floor * rate_floor)
    pressure = stiffness * density
    inertial = rate * grain_size / jnp.sqrt(pressure + press_floor)
    friction = mu_static + (mu_limit - mu_static) * inertial / (inertia_ref + inertial)
    twice = 2.0 * friction * pressure / rate
    sigma = jnp.stack(
        [
            twice * dxx - pressure,
            twice * dyy - pressure,
            twice * dzz - pressure,
            twice * dxy,
            twice * dxz,
            twice * dyz,
        ]
    )
    return jnp.where(keep, sigma, 0.0)


def two_hot(position, fraction, count, wrap):
    nodes = lax.broadcasted_iota(jnp.int32, (count, position.shape[0]), 0)
    upper = (position + 1) % count if wrap else position + 1
    lower_part = jnp.where(nodes == position[None, :], 1.0 - fraction[None, :], 0.0)
    upper_part = jnp.where(nodes == upper[None, :], fraction[None, :], 0.0)
    return lower_part + upper_part


def weight_tables(frac_b, local_b):
    cell_i = local_b // (NY * NZ)
    cell_j = local_b // NZ % NY
    cell_k = local_b % NZ
    along = two_hot(cell_i, frac_b[0], CX + 1, False)
    across = two_hot(cell_j, frac_b[1], NY, True)
    upward = two_hot(cell_k, frac_b[2], NZ, True)
    plane = (along[:, None, :] * across[None, :, :]).reshape((CX + 1) * NY, frac_b.shape[1])
    return (plane, upward)


def spread_block(accum, frac_b, vel_b, mass_b, local_b, alive):
    plane, upward = weight_tables(frac_b, local_b)
    held = jnp.where(alive, mass_b, 0.0)
    carried = jnp.stack([held, held * vel_b[0], held * vel_b[1], held * vel_b[2]])
    scaled = (carried[:, None, :] * plane[None]).reshape(4 * plane.shape[0], plane.shape[1])
    summed = lax.dot_general(
        scaled,
        upward,
        (((1,), (1,)), ((), ())),
        precision=highest,
        preferred_element_type=jnp.float32,
    )
    return accum + summed


def collect_block(frac_b, vel_b, local_b, alive, table_flat, step):
    plane, upward = weight_tables(frac_b, local_b)
    columns = jnp.dot(table_flat, upward, precision=highest, preferred_element_type=jnp.float32)
    picked = jnp.sum(columns.reshape(6, plane.shape[0], plane.shape[1]) * plane[None], axis=1)
    moved = picked[:3]
    change = picked[3:]
    fresh = jnp.where(alive, flip_share * (vel_b + change) + (1.0 - flip_share) * moved, 0.0)
    placed = jnp.where(alive, frac_b + step * moved, 0.0)
    speed = jnp.sqrt(jnp.sum(fresh * fresh, axis=0))
    return (placed, fresh, jnp.max(jnp.where(alive, speed, 0.0)))


def body(frac, velocity, mass, particle_cell, tile_count, time_step):
    step = time_step[0]
    slots_here = frac.shape[1]
    count = tile_count[0]
    layers = (CX + 1) * NY
    blocks = slots_here // PBLOCK

    def add_block(number, accum):
        start = number * PBLOCK
        alive = start + jnp.arange(PBLOCK, dtype=jnp.int32) < count
        return spread_block(
            accum,
            lax.dynamic_slice_in_dim(frac, start, PBLOCK, 1),
            lax.dynamic_slice_in_dim(velocity, start, PBLOCK, 1),
            lax.dynamic_slice_in_dim(mass, start, PBLOCK, 0),
            lax.dynamic_slice_in_dim(particle_cell, start, PBLOCK, 0),
            alive,
        )

    accum = lax.fori_loop(0, blocks, add_block, jnp.zeros((4 * layers, NZ), jnp.float32))
    spread = accum.reshape(4, CX + 1, NY, NZ)
    arriving = shifted(spread[:, CX], "gx", 1)
    nodes = jnp.concatenate([spread[:, :1] + arriving[:, None], spread[:, 1:CX]], axis=1)
    node_mass = nodes[0]
    momentum = nodes[1:]
    v_old = momentum / jnp.maximum(node_mass, mass_floor)
    upper_vel, upper_mass = shifted((v_old[:, 0], node_mass[0]), "gx", -1)
    ext_vel = jnp.concatenate([v_old, upper_vel[:, None]], axis=1)
    ext_mass = jnp.concatenate([node_mass, upper_mass[None]], axis=0)
    grads = [[cell_gradient(ext_vel[a], b) for b in range(3)] for a in range(3)]
    density = 0.125 * pair_up(pair_up(ext_mass[1:] + ext_mass[:-1], 1), 2)
    keep = lax.broadcasted_iota(jnp.int32, (CX, NY, NZ), 2) < NZ - 1
    sigma = stresses(grads, density, keep)
    lower = shifted(sigma[:, CX - 1], "gx", 1)
    force = node_forces(jnp.concatenate([lower[:, None], sigma], axis=1))
    gravity = jnp.array([gravity_x, 0.0, gravity_z], jnp.float32)[:, None, None, None]
    v_new = (momentum + step * (force + node_mass[None] * gravity)) / jnp.maximum(
        node_mass, mass_floor
    )
    above_bed = lax.broadcasted_iota(jnp.int32, (CX, NY, NZ), 2) > 0
    v_new = jnp.where(above_bed, v_new, 0.0)
    upper_new = shifted(v_new[:, 0], "gx", -1)
    ext_new = jnp.concatenate([v_new, upper_new[:, None]], axis=1)
    table_flat = jnp.concatenate([ext_new, ext_new - ext_vel]).reshape(6 * layers, NZ)

    def take_block(number, carry):
        placed_all, fresh_all, fastest = carry
        start = number * PBLOCK
        alive = start + jnp.arange(PBLOCK, dtype=jnp.int32) < count
        placed, fresh, top_block = collect_block(
            lax.dynamic_slice_in_dim(frac, start, PBLOCK, 1),
            lax.dynamic_slice_in_dim(velocity, start, PBLOCK, 1),
            lax.dynamic_slice_in_dim(particle_cell, start, PBLOCK, 0),
            alive,
            table_flat,
            step,
        )
        placed_all = lax.dynamic_update_slice_in_dim(placed_all, placed, start, 1)
        fresh_all = lax.dynamic_update_slice_in_dim(fresh_all, fresh, start, 1)
        return (placed_all, fresh_all, jnp.maximum(fastest, top_block))

    start_carry = (jnp.zeros_like(frac), jnp.zeros_like(velocity), jnp.zeros((), jnp.float32))
    new_frac, new_velocity, local_top = lax.fori_loop(0, blocks, take_block, start_carry)
    fastest = lax.pmax(local_top, "gx")
    next_step = (courant / (fastest + wave_speed)).reshape(1)
    return (new_frac, new_velocity, next_step)


def solution(mesh):
    placed = (
        P(None, ("runs", "gx")),
        P(None, ("runs", "gx")),
        P(("runs", "gx")),
        P(("runs", "gx")),
        P(("runs", "gx")),
        P("runs"),
    )
    return jax.shard_map(
        body,
        mesh=mesh,
        in_specs=placed,
        out_specs=(P(None, ("runs", "gx")), P(None, ("runs", "gx")), P("runs")),
        check_vma=False,
    )
```

profile of v0, /device:TPU:0, one launch (start us, length us, event | category | flops | bytes accessed | tf_op | source)
XLA Modules:
  0.0 215.3 jit_solution(16369442473663123069)
XLA Ops:
  0.6 57.5 %while.38 = (s32[]{:T(128)}, f32[384,128]{1,0:T(8,128)S(1)}, s32[]{:T(128)}, f32[16384]{0:T(1024)}, f32[3,16384]{1,0:T(4,128)}, /*index=5*/s32[16384]{0:T(1024)}...) while((s32[]{:T(128)}, f32[384,128]{1,0:T(8,128)S(1)}, ...), condition=%wide.region_1.2_spmd.clone, body=%wide.region_0.1_spmd.clone.sunk | while | flops 1210892288 | bytes 9298165 | solution.py:173
  2.1 1.0 broadcast_subtract_fusion.9
  3.1 1.4 fusion.116
  5.1 2.7 %convolution_add_fusion.2 = f32[384,128]{1,0:T(8,128)S(1)} fusion(f32[384,2048]{1,0:T(8,128)S(1)} %bitcast.185, f32[2048]{0:T(1024)S(1)} %bitcast.201, s32[2048]{0:T(1024)S(1)} %get-tuple-element.833, f32[2048]{0:T(1024)S(1)} %bitcast.200, s32[2048]{0:T(1024)S(1)} %get-tuple-element.835, f32[384,128]{1,0:T(8,128)S(1)} %get-tuple-element.850, ...), kind=kOutput, calls=%fused_computation.59.clone.1 | convolution fusion | flops 1209368576 | bytes 3571713 | tf_op jit(solution)/shard_map/while/body/eval_jaxpr/dot_general | solution.py:132
  9.3 1.0 broadcast_subtract_fusion.9
  10.3 1.4 fusion.116
  12.3 2.7 %convolution_add_fusion.2 = f32[384,128]{1,0:T(8,128)S(1)} fusion(f32[384,2048]{1,0:T(8,128)S(1)} %bitcast.185, f32[2048]{0:T(1024)S(1)} %bitcast.201, s32[2048]{0:T(1024)S(1)} %get-tuple-element.833, f32[2048]{0:T(1024)S(1)} %bitcast.200, s32[2048]{0:T(1024)S(1)} %get-tuple-element.835, f32[384,128]{1,0:T(8,128)S(1)} %get-tuple-element.850, ...), kind=kOutput, calls=%fused_computation.59.clone.1 | convolution fusion | flops 1209368576 | bytes 3571713 | tf_op jit(solution)/shard_map/while/body/eval_jaxpr/dot_general | solution.py:132
  16.5 1.0 broadcast_subtract_fusion.9
  17.5 1.4 fusion.116
  19.4 2.7 %convolution_add_fusion.2 = f32[384,128]{1,0:T(8,128)S(1)} fusion(f32[384,2048]{1,0:T(8,128)S(1)} %bitcast.185, f32[2048]{0:T(1024)S(1)} %bitcast.201, s32[2048]{0:T(1024)S(1)} %get-tuple-element.833, f32[2048]{0:T(1024)S(1)} %bitcast.200, s32[2048]{0:T(1024)S(1)} %get-tuple-element.835, f32[384,128]{1,0:T(8,128)S(1)} %get-tuple-element.850, ...), kind=kOutput, calls=%fused_computation.59.clone.1 | convolution fusion | flops 1209368576 | bytes 3571713 | tf_op jit(solution)/shard_map/while/body/eval_jaxpr/dot_general | solution.py:132
  23.7 1.0 broadcast_subtract_fusion.9
  24.7 1.4 fusion.116
  26.6 2.7 %convolution_add_fusion.2 = f32[384,128]{1,0:T(8,128)S(1)} fusion(f32[384,2048]{1,0:T(8,128)S(1)} %bitcast.185, f32[2048]{0:T(1024)S(1)} %bitcast.201, s32[2048]{0:T(1024)S(1)} %get-tuple-element.833, f32[2048]{0:T(1024)S(1)} %bitcast.200, s32[2048]{0:T(1024)S(1)} %get-tuple-element.835, f32[384,128]{1,0:T(8,128)S(1)} %get-tuple-element.850, ...), kind=kOutput, calls=%fused_computation.59.clone.1 | convolution fusion | flops 1209368576 | bytes 3571713 | tf_op jit(solution)/shard_map/while/body/eval_jaxpr/dot_general | solution.py:132
  30.9 1.0 broadcast_subtract_fusion.9
  31.9 1.4 fusion.116
  33.8 2.7 %convolution_add_fusion.2 = f32[384,128]{1,0:T(8,128)S(1)} fusion(f32[384,2048]{1,0:T(8,128)S(1)} %bitcast.185, f32[2048]{0:T(1024)S(1)} %bitcast.201, s32[2048]{0:T(1024)S(1)} %get-tuple-element.833, f32[2048]{0:T(1024)S(1)} %bitcast.200, s32[2048]{0:T(1024)S(1)} %get-tuple-element.835, f32[384,128]{1,0:T(8,128)S(1)} %get-tuple-element.850, ...), kind=kOutput, calls=%fused_computation.59.clone.1 | convolution fusion | flops 1209368576 | bytes 3571713 | tf_op jit(solution)/shard_map/while/body/eval_jaxpr/dot_general | solution.py:132
  38.0 1.0 broadcast_subtract_fusion.9
  39.1 1.4 fusion.116
  41.0 2.7 %convolution_add_fusion.2 = f32[384,128]{1,0:T(8,128)S(1)} fusion(f32[384,2048]{1,0:T(8,128)S(1)} %bitcast.185, f32[2048]{0:T(1024)S(1)} %bitcast.201, s32[2048]{0:T(1024)S(1)} %get-tuple-element.833, f32[2048]{0:T(1024)S(1)} %bitcast.200, s32[2048]{0:T(1024)S(1)} %get-tuple-element.835, f32[384,128]{1,0:T(8,128)S(1)} %get-tuple-element.850, ...), kind=kOutput, calls=%fused_computation.59.clone.1 | convolution fusion | flops 1209368576 | bytes 3571713 | tf_op jit(solution)/shard_map/while/body/eval_jaxpr/dot_general | solution.py:132
  45.2 1.0 broadcast_subtract_fusion.9
  46.2 1.4 fusion.116
  48.2 2.7 %convolution_add_fusion.2 = f32[384,128]{1,0:T(8,128)S(1)} fusion(f32[384,2048]{1,0:T(8,128)S(1)} %bitcast.185, f32[2048]{0:T(1024)S(1)} %bitcast.201, s32[2048]{0:T(1024)S(1)} %get-tuple-element.833, f32[2048]{0:T(1024)S(1)} %bitcast.200, s32[2048]{0:T(1024)S(1)} %get-tuple-element.835, f32[384,128]{1,0:T(8,128)S(1)} %get-tuple-element.850, ...), kind=kOutput, calls=%fused_computation.59.clone.1 | convolution fusion | flops 1209368576 | bytes 3571713 | tf_op jit(solution)/shard_map/while/body/eval_jaxpr/dot_general | solution.py:132
  52.4 1.0 broadcast_subtract_fusion.9
  53.4 1.4 fusion.116
  55.4 2.7 %convolution_add_fusion.2 = f32[384,128]{1,0:T(8,128)S(1)} fusion(f32[384,2048]{1,0:T(8,128)S(1)} %bitcast.185, f32[2048]{0:T(1024)S(1)} %bitcast.201, s32[2048]{0:T(1024)S(1)} %get-tuple-element.833, f32[2048]{0:T(1024)S(1)} %bitcast.200, s32[2048]{0:T(1024)S(1)} %get-tuple-element.835, f32[384,128]{1,0:T(8,128)S(1)} %get-tuple-element.850, ...), kind=kOutput, calls=%fused_computation.59.clone.1 | convolution fusion | flops 1209368576 | bytes 3571713 | tf_op jit(solution)/shard_map/while/body/eval_jaxpr/dot_general | solution.py:132
  59.3 6.3 %collective-permute-done = f32[4,32,128]{2,1,0:T(8,128)S(1)} collective-permute-done((f32[4,32,128]{2,1,0:T(8,128)S(1)}, f32[4,32,128]{2,1,0:T(8,128)S(1)}, u32[]{:S(2)}, u32[]{:S(2)}) %collective-permute-start) | collective-permute-done | bytes 65568 | tf_op jit(solution)/shard_map/ppermute | solution.py:31
  65.7 2.4 %collective-permute-start.1 = (f32[3,32,128]{2,1,0:T(8,128)S(1)}, f32[3,32,128]{2,1,0:T(8,128)S(1)}, u32[]{:S(2)}, u32[]{:S(2)}) collective-permute-start(f32[3,32,128]{2,1,0:T(8,128)S(1)} %slice_bitcast_fusion.3), channel_id=1, source_target_pairs={{0,15},{1,0},{2,1},{3,2},{4,3},{5,4},{6,5},{7,6},{8,7},{9,8},{10,9... | collective-permute-start | bytes 147464 | tf_op jit(solution)/shard_map/ppermute | solution.py:31
  68.3 1.6 collective-permute-done.1
  71.4 6.7 %collective-permute-done.3 = f32[6,32,128]{2,1,0:T(8,128)S(1)} collective-permute-done((f32[6,32,128]{2,1,0:T(8,128)S(1)}, f32[6,32,128]{2,1,0:T(8,128)S(1)}, u32[]{:S(2)}, u32[]{:S(2)}) %collective-permute-start.3) | collective-permute-done | bytes 98336 | tf_op jit(solution)/shard_map/ppermute | solution.py:31
  80.0 1.7 collective-permute-done.4
  81.9 96.3 %while.37 = (s32[]{:T(128)}, f32[3,16384]{1,0:T(4,128)S(1)}, f32[3,16384]{1,0:T(4,128)S(1)}, f32[]{:T(128)}, s32[]{:T(128)}, /*index=5*/f32[3,16384]{1,0:T(4,128...) while((s32[]{:T(128)}, f32[3,16384]{1,0:T(4,128)S(1)}, ...), condition=%wide.region_6.7_spmd, body=%wide.region_2.6_spmd.sunk | while | flops 1816381440 | bytes 12448031 | solution.py:216
  84.8 1.0 broadcast_subtract_fusion.8
  85.9 3.9 %fusion.113 = f32[2048,576]{0,1:T(8,128)S(1)} fusion(f32[576,128]{1,0:T(8,128)S(1)} %get-tuple-element.915, f32[2048]{0:T(1024)S(1)} %bitcast.192, s32[2048]{0:T(1024)S(1)} %get-tuple-element.794, f32[2048]{0:T(1024)S(1)} %bitcast.191, s32[2048]{0:T(1024)S(1)} %get-tuple-element.796), kind=kOutput, calls=%fused_computation.1.clone.1 | convolution fusion | flops 1813250048 | bytes 5046272 | tf_op jit(solution)/shard_map/while/body/eval_jaxpr/dot_general | solution.py:144
  90.5 1.5 multiply_reduce_fusion.5
  92.0 1.3 select_reduce_fusion.2
  96.8 1.0 broadcast_subtract_fusion.8
  98.0 3.9 %fusion.113 = f32[2048,576]{0,1:T(8,128)S(1)} fusion(f32[576,128]{1,0:T(8,128)S(1)} %get-tuple-element.915, f32[2048]{0:T(1024)S(1)} %bitcast.192, s32[2048]{0:T(1024)S(1)} %get-tuple-element.794, f32[2048]{0:T(1024)S(1)} %bitcast.191, s32[2048]{0:T(1024)S(1)} %get-tuple-element.796), kind=kOutput, calls=%fused_computation.1.clone.1 | convolution fusion | flops 1813250048 | bytes 5046272 | tf_op jit(solution)/shard_map/while/body/eval_jaxpr/dot_general | solution.py:144
  102.6 1.5 multiply_reduce_fusion.5
  104.1 1.3 select_reduce_fusion.2
  108.8 1.0 broadcast_subtract_fusion.8
  110.0 3.9 %fusion.113 = f32[2048,576]{0,1:T(8,128)S(1)} fusion(f32[576,128]{1,0:T(8,128)S(1)} %get-tuple-element.915, f32[2048]{0:T(1024)S(1)} %bitcast.192, s32[2048]{0:T(1024)S(1)} %get-tuple-element.794, f32[2048]{0:T(1024)S(1)} %bitcast.191, s32[2048]{0:T(1024)S(1)} %get-tuple-element.796), kind=kOutput, calls=%fused_computation.1.clone.1 | convolution fusion | flops 1813250048 | bytes 5046272 | tf_op jit(solution)/shard_map/while/body/eval_jaxpr/dot_general | solution.py:144
  114.6 1.5 multiply_reduce_fusion.5
  116.1 1.3 select_reduce_fusion.2
  120.9 1.0 broadcast_subtract_fusion.8
  122.0 3.9 %fusion.113 = f32[2048,576]{0,1:T(8,128)S(1)} fusion(f32[576,128]{1,0:T(8,128)S(1)} %get-tuple-element.915, f32[2048]{0:T(1024)S(1)} %bitcast.192, s32[2048]{0:T(1024)S(1)} %get-tuple-element.794, f32[2048]{0:T(1024)S(1)} %bitcast.191, s32[2048]{0:T(1024)S(1)} %get-tuple-element.796), kind=kOutput, calls=%fused_computation.1.clone.1 | convolution fusion | flops 1813250048 | bytes 5046272 | tf_op jit(solution)/shard_map/while/body/eval_jaxpr/dot_general | solution.py:144
  126.7 1.5 multiply_reduce_fusion.5
  128.1 1.3 select_reduce_fusion.2
  132.9 1.0 broadcast_subtract_fusion.8
  134.1 3.9 %fusion.113 = f32[2048,576]{0,1:T(8,128)S(1)} fusion(f32[576,128]{1,0:T(8,128)S(1)} %get-tuple-element.915, f32[2048]{0:T(1024)S(1)} %bitcast.192, s32[2048]{0:T(1024)S(1)} %get-tuple-element.794, f32[2048]{0:T(1024)S(1)} %bitcast.191, s32[2048]{0:T(1024)S(1)} %get-tuple-element.796), kind=kOutput, calls=%fused_computation.1.clone.1 | convolution fusion | flops 1813250048 | bytes 5046272 | tf_op jit(solution)/shard_map/while/body/eval_jaxpr/dot_general | solution.py:144
  138.7 1.5 multiply_reduce_fusion.5
  140.2 1.3 select_reduce_fusion.2
  145.0 1.0 broadcast_subtract_fusion.8
  146.1 3.9 %fusion.113 = f32[2048,576]{0,1:T(8,128)S(1)} fusion(f32[576,128]{1,0:T(8,128)S(1)} %get-tuple-element.915, f32[2048]{0:T(1024)S(1)} %bitcast.192, s32[2048]{0:T(1024)S(1)} %get-tuple-element.794, f32[2048]{0:T(1024)S(1)} %bitcast.191, s32[2048]{0:T(1024)S(1)} %get-tuple-element.796), kind=kOutput, calls=%fused_computation.1.clone.1 | convolution fusion | flops 1813250048 | bytes 5046272 | tf_op jit(solution)/shard_map/while/body/eval_jaxpr/dot_general | solution.py:144
  150.7 1.5 multiply_reduce_fusion.5
  152.2 1.3 select_reduce_fusion.2
  157.0 1.0 broadcast_subtract_fusion.8
  158.2 3.9 %fusion.113 = f32[2048,576]{0,1:T(8,128)S(1)} fusion(f32[576,128]{1,0:T(8,128)S(1)} %get-tuple-element.915, f32[2048]{0:T(1024)S(1)} %bitcast.192, s32[2048]{0:T(1024)S(1)} %get-tuple-element.794, f32[2048]{0:T(1024)S(1)} %bitcast.191, s32[2048]{0:T(1024)S(1)} %get-tuple-element.796), kind=kOutput, calls=%fused_computation.1.clone.1 | convolution fusion | flops 1813250048 | bytes 5046272 | tf_op jit(solution)/shard_map/while/body/eval_jaxpr/dot_general | solution.py:144
  162.8 1.5 multiply_reduce_fusion.5
  164.3 1.3 select_reduce_fusion.2
  169.0 1.0 broadcast_subtract_fusion.8
  170.2 3.9 %fusion.113 = f32[2048,576]{0,1:T(8,128)S(1)} fusion(f32[576,128]{1,0:T(8,128)S(1)} %get-tuple-element.915, f32[2048]{0:T(1024)S(1)} %bitcast.192, s32[2048]{0:T(1024)S(1)} %get-tuple-element.794, f32[2048]{0:T(1024)S(1)} %bitcast.191, s32[2048]{0:T(1024)S(1)} %get-tuple-element.796), kind=kOutput, calls=%fused_computation.1.clone.1 | convolution fusion | flops 1813250048 | bytes 5046272 | tf_op jit(solution)/shard_map/while/body/eval_jaxpr/dot_general | solution.py:144
  174.8 1.5 multiply_reduce_fusion.5
  176.3 1.3 select_reduce_fusion.2
  178.3 35.2 %pmax.7 = f32[]{:T(128)} all-reduce(f32[]{:T(128)} %get-tuple-element.508), channel_id=1, replica_groups=mesh['runs'=2,'gx'=16] {'gx'}, use_global_device_ids=true, to_apply=%region_7.8 | all-reduce | flops 1 | bytes 8 | tf_op jit(solution)/shard_map/pmax | solution.py:217
  (234 shorter events, 49.1 us)
Async XLA Ops:
  58.1 7.5 %collective-permute-start = (f32[4,32,128]{2,1,0:T(8,128)S(1)}, f32[4,32,128]{2,1,0:T(8,128)S(1)}, u32[]{:S(2)}, u32[]{:S(2)}) collective-permute-start(f32[4,32,128]{2,1,0:T(8,128)S(1)} %slice_bitcast_fusion.1), channel_id=1, source_target_pairs={{0,1},{1,2},{2,3},{3,4},{4,5},{5,6},{6,7},{7,8},{8,9},{9,10},{10,1... | collective-permute-start | bytes 196616 | tf_op jit(solution)/shard_map/ppermute | solution.py:31
  65.6 2.6 %collective-permute-start.2 = (f32[32,128]{1,0:T(8,128)S(1)}, f32[32,128]{1,0:T(8,128)S(1)}, u32[]{:S(2)}, u32[]{:S(2)}) collective-permute-start(f32[32,128]{1,0:T(8,128)S(1)} %slice_bitcast_fusion.4), channel_id=1, source_target_pairs={{0,15},{1,0},{2,1},{3,2},{4,3},{5,4},{6,5},{7,6},{8,7},{9,8},{10,9... | collective-permute-start | bytes 49160 | tf_op jit(solution)/shard_map/ppermute | solution.py:31
  65.7 4.2 %collective-permute-start.1 = (f32[3,32,128]{2,1,0:T(8,128)S(1)}, f32[3,32,128]{2,1,0:T(8,128)S(1)}, u32[]{:S(2)}, u32[]{:S(2)}) collective-permute-start(f32[3,32,128]{2,1,0:T(8,128)S(1)} %slice_bitcast_fusion.3), channel_id=1, source_target_pairs={{0,15},{1,0},{2,1},{3,2},{4,3},{5,4},{6,5},{7,6},{8,7},{9,8},{10,9... | collective-permute-start | bytes 147464 | tf_op jit(solution)/shard_map/ppermute | solution.py:31
  70.9 9.0 %copy-start.2 = (f32[3]{0:T(128)S(1)}, f32[3]{0:T(128)}, u32[]{:S(2)}) copy-start(f32[3]{0:T(128)} %constant.435.clone) | copy-start | bytes 40
  71.3 6.8 %collective-permute-start.3 = (f32[6,32,128]{2,1,0:T(8,128)S(1)}, f32[6,32,128]{2,1,0:T(8,128)S(1)}, u32[]{:S(2)}, u32[]{:S(2)}) collective-permute-start(f32[6,32,128]{2,1,0:T(8,128)S(1)} %slice_bitcast_fusion), channel_id=1, source_target_pairs={{0,1},{1,2},{2,3},{3,4},{4,5},{5,6},{6,7},{7,8},{8,9},{9,10},{10,1... | collective-permute-start | bytes 294920 | tf_op jit(solution)/shard_map/ppermute | solution.py:31
  80.0 1.8 collective-permute-start.4
  178.2 35.9 %copy-start = (f32[3,16384]{1,0:T(4,128)}, f32[3,16384]{1,0:T(4,128)S(1)}, u32[]{:S(2)}) copy-start(f32[3,16384]{1,0:T(4,128)S(1)} %get-tuple-element.503) | copy-start | bytes 589828
  178.3 35.9 %copy-start.1 = (f32[3,16384]{1,0:T(4,128)}, f32[3,16384]{1,0:T(4,128)S(1)}, u32[]{:S(2)}) copy-start(f32[3,16384]{1,0:T(4,128)S(1)} %get-tuple-element.502) | copy-start | bytes 589828
where the time goes:
time: 220 us; the launch traced here: 215 us
  other arithmetic  95.3 us (43%)
  matrix products  53.3 us (24%)
  blocking collectives  35.2 us (16%)
  waiting for transfers between devices  16.4 us (7%)
  loops' own time  6.53 us (3%)
  between operations  3.62 us (2%)
  starting transfers between devices  3.12 us (1%)
    pmax x1, blocking collectives, body(): fastest = lax.pmax(local_top, 'gx')  35.2 us
    dot_general x8, matrix products, collect_block(): jnp.dot(table_flat, upward, precision=highest, preferred_element_type=jnp...  31.4 us
    select_n x32, other arithmetic, two_hot(): upper = (position + 1) % count if wrap else position + 1  23.2 us
    dot_general x8, matrix products, spread_block(): lax.dot_general(scaled, upward, (((1,), (1,)), ((), ())), precision=highe...  22 us
    ppermute x5, waiting for transfers between devices, shifted(): lax.ppermute(array, axis, [(i, (i + by) % devices) for i in range(devices)])  16.4 us
    sub x16, other arithmetic, two_hot(): 1.0 - fraction[None, :]  16 us
    reduce_sum x8, other arithmetic, collect_block(): speed = jnp.sqrt(jnp.sum(fresh * fresh, axis=0))  11.9 us
    mul x8, other arithmetic, spread_block(): held * vel_b[0]  10.8 us
  transfers between devices with their start and end apart: 5, of which 4 were waited for; matrix products, arithmetic and copies ran while one was open for 0% of the time, Pallas kernels for 0%

commit v1 on v0

v1 whole, which is shorter than its diff:
```python
import functools

import jax
import jax.numpy as jnp
from jax import lax
from jax.experimental import pallas as pl
from jax.experimental.pallas import tpu as pltpu
from jax.sharding import PartitionSpec as P

CX = 2
NY = 32
NZ = 128
ROWS = CX * NY
BLOCK = 256
UNROLL = 8
SPREAD = 32
TABLE = 64

mass_floor = 0.25
stiffness = 2.0
press_floor = 1.0
grain_size = 0.5
inertia_ref = 0.3
mu_static = 0.38
mu_limit = 0.64
rate_floor = 0.5
gravity = (0.5, 0.0, -0.866)
flip_share = 0.95
courant = 0.4
wave_speed = 2.0
components = ((0, 3, 4), (3, 1, 5), (4, 5, 2))
f32 = jnp.float32
bf16 = jnp.bfloat16


def shifted(array, axis, by):
    devices = lax.axis_size(axis)
    return lax.ppermute(array, axis, [(i, (i + by) % devices) for i in range(devices)])


def visit_list(particle_cell, count):
    slots = particle_cell.shape[0]
    blocks = slots // BLOCK
    size = blocks + ROWS
    number = jnp.arange(blocks, dtype=jnp.int32)
    cells = particle_cell.reshape(blocks, BLOCK)
    live = jnp.arange(slots, dtype=jnp.int32).reshape(blocks, BLOCK) < count
    first = cells[:, 0] // NZ
    last = jnp.max(jnp.where(live, cells, 0), axis=1) // NZ
    visits = jnp.where(number * BLOCK < count, last - first + 1, 0)
    before = number[:, None] < number[None, :]
    starts = jnp.sum(jnp.where(before, visits[:, None], 0), axis=0)
    total = jnp.sum(visits)
    order = jnp.arange(size, dtype=jnp.int32)
    inside = (starts[None, :] <= order[:, None]) & (order[:, None] < (starts + visits)[None, :])
    block = jnp.sum(jnp.where(inside, number[None, :], 0), axis=1)
    row = jnp.sum(jnp.where(inside, (first - starts)[None, :], 0), axis=1) + order
    row = jnp.where(order < total, row, ROWS)
    return block, row, total.reshape(1)


def split_pair(values):
    high = values.astype(bf16)
    low = (values - high.astype(f32)).astype(bf16)
    return high, low


def one_hot(cells_ref, block, row):
    rel = cells_ref[pl.ds(block * 2, 2), :] - row * NZ
    nodes = lax.broadcasted_iota(jnp.int32, (NZ, 128), 0)
    halves = [jnp.where(nodes == rel[h : h + 1, :], 1.0, 0.0) for h in range(2)]
    return jnp.concatenate(halves, axis=1).astype(bf16)


def pair_lines(ref, block):
    both = ref[pl.ds(block * 2, 2), :]
    return jnp.concatenate([both[0:1, :], both[1:2, :]], axis=1)


def spread_kernel(
    count_ref, block_ref, row_ref, total_ref, frac_ref, vel_ref, mass_ref, cells_ref,
    low_ref, high_ref, q_ref, acc_ref,
):
    blocks = frac_ref.shape[1] // BLOCK
    count = count_ref[0]
    acc_ref[...] = jnp.zeros_like(acc_ref)
    corner = lax.broadcasted_iota(jnp.int32, (8, BLOCK), 0)
    upper = [(corner // part) % 2 == 1 for part in (4, 2, 1)]
    lane = lax.broadcasted_iota(jnp.int32, (1, BLOCK), 1)

    def prepare(block, carry):
        at = pl.multiple_of(block * BLOCK, BLOCK)
        frac = frac_ref[:, pl.ds(at, BLOCK)]
        vel = vel_ref[:, pl.ds(at, BLOCK)]
        mass = pair_lines(mass_ref, block)
        held = jnp.where(at + lane < count, mass, 0.0)
        parts = [
            jnp.where(upper[d], frac[d : d + 1, :], 1.0 - frac[d : d + 1, :]) for d in range(3)
        ]
        weight = parts[0] * parts[1] * parts[2] * held
        carried = jnp.concatenate([weight] + [weight * vel[a : a + 1, :] for a in range(3)], axis=0)
        high, low = split_pair(carried)
        q_ref[pl.ds(block, 1)] = jnp.concatenate([high, low], axis=0)[None]
        return carry

    lax.fori_loop(0, blocks, prepare, 0, unroll=4)

    def visit(group, carry):
        found = []
        for u in range(UNROLL):
            v = group * UNROLL + u
            block = block_ref[v]
            row = row_ref[v]
            hot = one_hot(cells_ref, block, row)
            both = lax.dot_general(
                q_ref[pl.ds(block, 1)][0], hot, (((1,), (1,)), ((), ())), preferred_element_type=f32
            )
            found.append((row, both[:SPREAD] + both[SPREAD:]))
        for row, part in found:
            at = pl.ds(pl.multiple_of(row * SPREAD, SPREAD), SPREAD)
            acc_ref[at, :] += part
        return carry

    lax.fori_loop(0, (total_ref[0] + UNROLL - 1) // UNROLL, visit, 0)

    for field in range(4):
        layers = [None] * 3
        for i in range(CX):
            for a in range(2):
                summed = None
                for b in range(2):
                    line = None
                    for c in range(2):
                        start = i * NY * SPREAD + field * 8 + a * 4 + b * 2 + c
                        got = acc_ref[pl.ds(start, NY, stride=SPREAD), :]
                        line = got if c == 0 else line + pltpu.roll(got, 1, 1)
                    summed = line if b == 0 else summed + pltpu.roll(line, 1, 0)
                there = layers[i + a]
                layers[i + a] = summed if there is None else there + summed
        for l in range(2):
            low_ref[field * 2 + l] = layers[l]
            high_ref[field * 2 + l] = layers[l + 1]


def pair_up(field, axis):
    return field + pltpu.roll(field, field.shape[axis] - 1, axis)


def step_up(field, axis):
    return pltpu.roll(field, field.shape[axis] - 1, axis) - field


def pair_down(field, axis):
    return field + pltpu.roll(field, 1, axis)


def step_down(field, axis):
    return field - pltpu.roll(field, 1, axis)


def cell_stress(vel_lo, vel_hi, mass_lo, mass_hi, keep):
    grads = []
    for a in range(3):
        diff = vel_hi[a] - vel_lo[a]
        both = vel_hi[a] + vel_lo[a]
        grads.append(
            [
                0.25 * pair_up(pair_up(diff, 0), 1),
                0.25 * pair_up(step_up(both, 0), 1),
                0.25 * step_up(pair_up(both, 0), 1),
            ]
        )
    density = 0.125 * pair_up(pair_up(mass_hi + mass_lo, 0), 1)
    dxx = grads[0][0]
    dyy = grads[1][1]
    dzz = grads[2][2]
    dxy = 0.5 * (grads[0][1] + grads[1][0])
    dxz = 0.5 * (grads[0][2] + grads[2][0])
    dyz = 0.5 * (grads[1][2] + grads[2][1])
    second = dxx * dxx + dyy * dyy + dzz * dzz + 2.0 * (dxy * dxy + dxz * dxz + dyz * dyz)
    rate = jnp.sqrt(2.0 * second + rate_floor * rate_floor)
    pressure = stiffness * density
    inertial = rate * grain_size / jnp.sqrt(pressure + press_floor)
    friction = mu_static + (mu_limit - mu_static) * inertial / (inertia_ref + inertial)
    twice = 2.0 * friction * pressure / rate
    sigma = [
        twice * dxx - pressure,
        twice * dyy - pressure,
        twice * dzz - pressure,
        twice * dxy,
        twice * dxz,
        twice * dyz,
    ]
    return [jnp.where(keep, s, 0.0) for s in sigma]


def node_force(lower, upper):
    force = []
    for a in range(3):
        sx, sy, sz = (components[a][b] for b in range(3))
        along = pair_down(pair_down(upper[sx] - lower[sx], 0), 1)
        across = step_down(pair_down(upper[sy] + lower[sy], 1), 0)
        upward = step_down(pair_down(upper[sz] + lower[sz], 0), 1)
        force.append(0.25 * (along + across + upward))
    return force


def collect_kernel(
    count_ref, block_ref, row_ref, total_ref, step_ref,
    low_ref, high_ref, left_ref, right_ref, frac_ref, vel_ref, cells_ref,
    new_frac_ref, new_vel_ref, top_ref, tab_ref, out_ref,
):
    blocks = frac_ref.shape[1] // BLOCK
    count = count_ref[0]
    step = step_ref[0]
    nodes = [
        [left_ref[f * 2] for f in range(4)],
        [low_ref[f * 2] + left_ref[f * 2 + 1] for f in range(4)],
        [low_ref[f * 2 + 1] for f in range(4)],
        [high_ref[f * 2 + 1] + right_ref[f * 2] for f in range(4)],
        [right_ref[f * 2 + 1] for f in range(4)],
    ]
    height = lax.broadcasted_iota(jnp.int32, (NY, NZ), 1)
    keep = height < NZ - 1
    above_bed = height > 0
    floor = [jnp.maximum(layer[0], mass_floor) for layer in nodes]
    v_old = [[layer[1 + a] / floor[l] for a in range(3)] for l, layer in enumerate(nodes)]
    sigma = [
        cell_stress(v_old[l], v_old[l + 1], nodes[l][0], nodes[l + 1][0], keep) for l in range(4)
    ]
    tab_ref[...] = jnp.zeros_like(tab_ref)
    for l in range(1, 4):
        force = node_force(sigma[l - 1], sigma[l])
        for a in range(3):
            fresh = (
                nodes[l][1 + a] + step * (force[a] + nodes[l][0] * gravity[a])
            ) / floor[l]
            fresh = jnp.where(above_bed, fresh, 0.0)
            for field, value in ((a, fresh - flip_share * v_old[l][a]), (4 + a, step * fresh)):
                for b in range(2):
                    line = value if b == 0 else pltpu.roll(value, NY - 1, 0)
                    for c in range(2):
                        put = line if c == 0 else pltpu.roll(line, NZ - 1, 1)
                        for i in range(CX):
                            corner_a = l - 1 - i
                            if corner_a not in (0, 1):
                                continue
                            corner = corner_a * 4 + b * 2 + c
                            start = i * NY * TABLE + corner * 8 + field
                            tab_ref[pl.ds(start, NY, stride=TABLE), :] = put

    out_ref[...] = jnp.zeros_like(out_ref)

    def visit(group, carry):
        found = []
        for u in range(UNROLL):
            v = group * UNROLL + u
            block = block_ref[v]
            row = row_ref[v]
            hot = one_hot(cells_ref, block, row)
            at = pl.ds(pl.multiple_of(jnp.minimum(row, ROWS - 1) * TABLE, TABLE), TABLE)
            high, low = split_pair(tab_ref[at, :])
            both = jnp.dot(jnp.concatenate([high, low], axis=0), hot, preferred_element_type=f32)
            value = both[:TABLE] + both[TABLE:]
            frac = frac_ref[:, pl.ds(pl.multiple_of(block * BLOCK, BLOCK), BLOCK)]
            corners = [value[8 * k : 8 * k + 8] for k in range(8)]
            for d in (2, 1, 0):
                share = frac[d : d + 1, :]
                corners = [
                    corners[k] + share * (corners[k + 1] - corners[k])
                    for k in range(0, len(corners), 2)
                ]
            found.append((block, corners[0]))
        for block, part in found:
            out_ref[pl.ds(block, 1)] += part[None]
        return carry

    lax.fori_loop(0, (total_ref[0] + UNROLL - 1) // UNROLL, visit, 0)

    lane = lax.broadcasted_iota(jnp.int32, (1, BLOCK), 1)

    def finish(block, top):
        at = pl.multiple_of(block * BLOCK, BLOCK)
        alive = at + lane < count
        got = out_ref[pl.ds(block, 1)][0]
        fresh = jnp.where(alive, flip_share * vel_ref[:, pl.ds(at, BLOCK)] + got[0:3], 0.0)
        new_vel_ref[:, pl.ds(at, BLOCK)] = fresh
        placed = jnp.where(alive, frac_ref[:, pl.ds(at, BLOCK)] + got[4:7], 0.0)
        new_frac_ref[:, pl.ds(at, BLOCK)] = placed
        square = fresh[0:1] * fresh[0:1] + fresh[1:2] * fresh[1:2] + fresh[2:3] * fresh[2:3]
        return jnp.maximum(top, square)

    top = lax.fori_loop(0, blocks, finish, jnp.zeros((1, BLOCK), f32), unroll=4)
    top = jnp.sqrt(jnp.max(top, axis=1, keepdims=True))
    top_ref[...] = jnp.broadcast_to(top, top_ref.shape)


def largest(value, axis):
    devices = lax.axis_size(axis)
    reach = 1
    while reach < devices:
        if devices & (devices - 1) == 0:
            pairs = [(i, i ^ reach) for i in range(devices)]
        else:
            pairs = [(i, (i + reach) % devices) for i in range(devices)]
        value = jnp.maximum(value, lax.ppermute(value, axis, pairs))
        reach *= 2
    return value


smem = pl.BlockSpec(memory_space=pltpu.SMEM)
vmem = pl.BlockSpec(memory_space=pltpu.VMEM)


def body(frac, velocity, mass, particle_cell, tile_count, time_step):
    slots = frac.shape[1]
    blocks = slots // BLOCK
    count = tile_count[0]
    block, row, total = visit_list(particle_cell, count)
    mass_rows = mass.reshape(slots // 128, 128)
    cell_rows = particle_cell.reshape(slots // 128, 128)
    layer_pair = jax.ShapeDtypeStruct((8, NY, NZ), f32)
    low, high = pl.pallas_call(
        spread_kernel,
        out_shape=(layer_pair, layer_pair),
        in_specs=[smem] * 4 + [vmem] * 4,
        out_specs=(vmem, vmem),
        scratch_shapes=[
            pltpu.VMEM((blocks, 2 * SPREAD, BLOCK), bf16),
            pltpu.VMEM(((ROWS + 1) * SPREAD, NZ), f32),
        ],
        compiler_params=pltpu.CompilerParams(vmem_limit_bytes=32 * 1024 * 1024),
        name="spread",
    )(tile_count, block, row, total, frac, velocity, mass_rows, cell_rows)
    from_left = shifted(high, "gx", 1)
    from_right = shifted(low, "gx", -1)
    new_frac, new_velocity, top = pl.pallas_call(
        collect_kernel,
        out_shape=(
            jax.ShapeDtypeStruct(frac.shape, f32),
            jax.ShapeDtypeStruct(velocity.shape, f32),
            jax.ShapeDtypeStruct((8, 128), f32),
        ),
        in_specs=[smem] * 5 + [vmem] * 7,
        out_specs=(vmem, vmem, vmem),
        scratch_shapes=[
            pltpu.VMEM((ROWS * TABLE, NZ), f32),
            pltpu.VMEM((blocks, 8, BLOCK), f32),
        ],
        compiler_params=pltpu.CompilerParams(vmem_limit_bytes=32 * 1024 * 1024),
        name="collect",
    )(
        tile_count, block, row, total, time_step,
        low, high, from_left, from_right, frac, velocity, cell_rows,
    )
    fastest = largest(top[0, :1], "gx")
    next_step = courant / (fastest + wave_speed)
    return (new_frac, new_velocity, next_step)


def solution(mesh):
    placed = (
        P(None, ("runs", "gx")),
        P(None, ("runs", "gx")),
        P(("runs", "gx")),
        P(("runs", "gx")),
        P(("runs", "gx")),
        P("runs"),
    )
    return jax.shard_map(
        body,
        mesh=mesh,
        in_specs=placed,
        out_specs=(P(None, ("runs", "gx")), P(None, ("runs", "gx")), P("runs")),
        check_vma=False,
    )
```

time: 220 us -> 51.9 us (0.24); the launches traced: 215 us -> 52.4 us
  other arithmetic: 95.3 us -> 1.89 us
  matrix products: 53.3 us -> 0 us
  blocking collectives: 35.2 us -> 0 us
  Pallas kernels: 0 us -> 15.6 us
  starting transfers between devices: 3.12 us -> 9.91 us
  loops' own time: 6.53 us -> 0 us
  between operations: 3.62 us -> 6.63 us
    dot_general x16 -> x0, matrix products: 53.3 us -> none  [the longest x8 31.4 us: collect_block(): jnp.dot(table_flat, upward, precision=highest, preferred_element_type=jnp...]
    pmax x1 -> x0, blocking collectives: 35.2 us -> none  [body(): fastest = lax.pmax(local_top, 'gx')]
    select_n x34 -> x1, other arithmetic: 23.3 us -> 0.7 us  [visit_list(): row = jnp.where(order < total, row, ROWS)]
    reduce_sum x16 -> x3, other arithmetic: 17.3 us -> 0.93 us  [the longest x1 0.72 us: visit_list(): total = jnp.sum(visits)]
    sub x19 -> x0, other arithmetic: 16 us -> none  [the longest x16 16 us: two_hot(): 1.0 - fraction[None, :]]
    pallas_call x0 -> x2, Pallas kernels: none -> 15.6 us  [the longest x1 8.64 us: body(): pl.pallas_call(collect_kernel, out_shape=(jax.ShapeDtypeStruct(frac.shape...]
    mul x40 -> x0, other arithmetic: 14.9 us -> none  [the longest x8 10.8 us: spread_block(): held * vel_b[0]]
    ppermute x5 -> x2, waiting for transfers between devices: 16.4 us -> 6.43 us  [shifted(): lax.ppermute(array, axis, [(i, (i + by) % devices) for i in range(devices)])]
  transfers between devices with their start and end apart: 5 -> 6, of which waited for: 4 -> 6; matrix products, arithmetic and copies ran while one was open for 0% -> 0% of each run, Pallas kernels for 0% -> 0%
where the time goes in v1:
time: 51.9 us; the launch traced here: 52.4 us
  Pallas kernels  15.6 us (30%)
  waiting for transfers between devices  15.1 us (29%)
  starting transfers between devices  9.91 us (19%)
  between operations  6.63 us (13%)
  local copies, waits for them, and re-layouts  3.26 us (6%)
  other arithmetic  1.89 us (4%)
    ppermute x4, waiting for transfers between devices, largest(): value = jnp.maximum(value, lax.ppermute(value, axis, pairs))  8.7 us
    pallas_call x1, Pallas kernels, body(): pl.pallas_call(collect_kernel, out_shape=(jax.ShapeDtypeStruct(frac.shape...  8.64 us
    pallas_call x1, Pallas kernels, body(): pl.pallas_call(spread_kernel, out_shape=(layer_pair, layer_pair), in_spec...  6.92 us
    ppermute x2, waiting for transfers between devices, shifted(): lax.ppermute(array, axis, [(i, (i + by) % devices) for i in range(devices)])  6.43 us
    ppermute x2, starting transfers between devices, shifted(): lax.ppermute(array, axis, [(i, (i + by) % devices) for i in range(devices)])  5.81 us
    ppermute x4, starting transfers between devices, largest(): value = jnp.maximum(value, lax.ppermute(value, axis, pairs))  4.11 us
    unnamed x8, local copies, waits for them, and re-layouts  1.79 us
  transfers between devices with their start and end apart: 6, of which 6 were waited for; matrix products, arithmetic and copies ran while one was open for 0% of the time, Pallas kernels for 0%

profile of v1, /device:TPU:0, one launch (start us, length us, event | category | flops | bytes accessed | tf_op | source)
XLA Modules:
  0.0 52.4 jit_solution(1966279245311772855)
XLA Ops:
  0.6 0.0 copy-start
  1.3 0.9 %reshape.156 = s32[64,256]{1,0:T(8,128)S(1)} reshape(s32[16384]{0:T(1024)} %param.9) | data formatting | bytes 131072 | tf_op jit(solution)/shard_map/reshape | solution.py:46
  2.2 0.1 select_reduce_fusion
  2.3 0.0 copy-start.2
  2.3 0.1 copy.17
  2.4 0.1 slice_reduce_fusion
  2.6 0.1 select_reduce_fusion.3
  2.7 0.7 %fusion.9 = (s32[]{:T(128)}, s32[64]{0:T(128)S(1)}, s32[64]{0:T(128)S(1)}) fusion(s32[64]{0:T(128)S(1)} %select_reduce_fusion, s32[]{:T(128)} %bitcast.8, s32[64]{0:T(128)S(1)} %get-tuple-element.13), kind=kLoop, calls=%fused_computation.39 | loop fusion | flops 2303 | bytes 1032 | tf_op jit(solution)/shard_map/reduce_sum | solution.py:53
  3.4 0.1 select_reduce_fusion.1
  3.5 0.7 %compare_select_fusion.row_ref = s32[128]{0:T(128)S(1)} fusion(s32[128]{0:T(128)S(1)} %get-tuple-element.15, s32[]{:T(128)} %get-tuple-element.17), kind=kLoop, calls=%fused_computation.29 | loop fusion | flops 384 | bytes 1028 | tf_op jit(solution)/shard_map/jit(_where)/select_n | solution.py:58
  4.2 0.0 copy-done
  4.2 0.0 copy-done.2
  4.2 0.0 copy-start.1
  4.2 0.9 %copy-done.1 = f32[3,16384]{1,0:T(4,128)S(1)} copy-done((f32[3,16384]{1,0:T(4,128)S(1)}, f32[3,16384]{1,0:T(4,128)}, u32[]{:S(2)}) %copy-start.1) | copy-done | bytes 196632
  5.2 0.0 copy-start.3
  5.2 0.8 %copy-done.3 = f32[16384]{0:T(1024)S(1)} copy-done((f32[16384]{0:T(1024)S(1)}, f32[16384]{0:T(1024)}, u32[]{:S(2)}) %copy-start.3) | copy-done | bytes 65560
  6.0 6.9 %spread.1 = (f32[8,32,128]{2,1,0:T(8,128)S(1)}, f32[8,32,128]{2,1,0:T(8,128)S(1)}) custom-call(s32[1]{0:T(128)} %copy.21.count_ref, s32[128]{0:T(128)S(1)} %get-tuple-element.16.block_ref, s32[128]{0:T(128)S(1)} %compare_select_fusion.row_ref, s32[1]{0:T(128)} %bitcast.2.total_ref, f32[3,16384]{1,0:T(4,128)S(1)} %copy-done, f32[3,16384]{1,0:T(4,128)S(1)} %copy-done.1, ...), custom_call_target="tpu_custom_call" | custom-call | tf_op jit(solution)/shard_map/spread/pallas_call | solution.py:323
  12.9 5.8 %collective-permute-start.1 = (f32[8,32,128]{2,1,0:T(8,128)S(1)}, f32[8,32,128]{2,1,0:T(8,128)S(1)}, u32[]{:S(2)}, u32[]{:S(2)}) collective-permute-start(f32[8,32,128]{2,1,0:T(8,128)S(1)} %get-tuple-element.8.low_ref), channel_id=1, source_target_pairs={{0,15},{1,0},{2,1},{3,2},{4,3},{5,4},{6,5},{7,6},{8,7},{9,8},{10,9... | collective-permute-start | bytes 393224 | tf_op jit(solution)/shard_map/ppermute | solution.py:38
  18.7 0.0 collective-permute-start
  19.4 1.9 %collective-permute-done.1.right_ref = f32[8,32,128]{2,1,0:T(8,128)S(1)} collective-permute-done((f32[8,32,128]{2,1,0:T(8,128)S(1)}, f32[8,32,128]{2,1,0:T(8,128)S(1)}, u32[]{:S(2)}, u32[]{:S(2)}) %collective-permute-start.1) | collective-permute-done | bytes 131104 | tf_op jit(solution)/shard_map/ppermute | solution.py:38
  21.3 4.6 %collective-permute-done.left_ref = f32[8,32,128]{2,1,0:T(8,128)S(1)} collective-permute-done((f32[8,32,128]{2,1,0:T(8,128)S(1)}, f32[8,32,128]{2,1,0:T(8,128)S(1)}, u32[]{:S(2)}, u32[]{:S(2)}) %collective-permute-start) | collective-permute-done | bytes 131104 | tf_op jit(solution)/shard_map/ppermute | solution.py:38
  25.8 8.6 %collect.1 = (f32[3,16384]{1,0:T(4,128)}, f32[3,16384]{1,0:T(4,128)}, f32[8,128]{1,0:T(8,128)S(1)}) custom-call(s32[1]{0:T(128)} %copy.21.count_ref, s32[128]{0:T(128)S(1)} %get-tuple-element.16.block_ref, s32[128]{0:T(128)S(1)} %compare_select_fusion.row_ref, s32[1]{0:T(128)} %bitcast.2.total_ref, f32[1]{0:T(128)S(6)} %copy.22.step_ref, ...), custom_call_target="tpu_custom_call" | custom-call | tf_op jit(solution)/shard_map/collect/pallas_call | solution.py:337
  34.5 0.5 slice.7
  35.0 0.0 collective-permute-start.2
  35.0 1.2 %collective-permute-done.2 = f32[1]{0:T(128)} collective-permute-done((f32[1]{0:T(128)}, f32[1]{0:T(128)}, u32[]{:S(2)}, u32[]{:S(2)}) %collective-permute-start.2) | collective-permute-done | bytes 36 | tf_op jit(solution)/shard_map/ppermute | solution.py:306
  37.6 1.4 %collective-permute-start.3 = (f32[1]{0:T(128)}, f32[1]{0:T(128)}, u32[]{:S(2)}, u32[]{:S(2)}) collective-permute-start(f32[1]{0:T(128)} %max.12), channel_id=1, source_target_pairs={{0,2},{1,3},{2,0},{3,1},{4,6},{5,7},{6,4},{7,5},{8,10},{9,11},{10,... | collective-permute-start | bytes 20 | tf_op jit(solution)/shard_map/ppermute | solution.py:306
  38.9 2.2 %collective-permute-done.3 = f32[1]{0:T(128)} collective-permute-done((f32[1]{0:T(128)}, f32[1]{0:T(128)}, u32[]{:S(2)}, u32[]{:S(2)}) %collective-permute-start.3) | collective-permute-done | bytes 36 | tf_op jit(solution)/shard_map/ppermute | solution.py:306
  41.8 1.4 %collective-permute-start.4 = (f32[1]{0:T(128)}, f32[1]{0:T(128)}, u32[]{:S(2)}, u32[]{:S(2)}) collective-permute-start(f32[1]{0:T(128)} %max.13), channel_id=1, source_target_pairs={{0,4},{1,5},{2,6},{3,7},{4,0},{5,1},{6,2},{7,3},{8,12},{9,13},{10,... | collective-permute-start | bytes 20 | tf_op jit(solution)/shard_map/ppermute | solution.py:306
  43.2 2.2 %collective-permute-done.4 = f32[1]{0:T(128)} collective-permute-done((f32[1]{0:T(128)}, f32[1]{0:T(128)}, u32[]{:S(2)}, u32[]{:S(2)}) %collective-permute-start.4) | collective-permute-done | bytes 36 | tf_op jit(solution)/shard_map/ppermute | solution.py:306
  46.1 1.4 %collective-permute-start.5 = (f32[1]{0:T(128)}, f32[1]{0:T(128)}, u32[]{:S(2)}, u32[]{:S(2)}) collective-permute-start(f32[1]{0:T(128)} %max.14), channel_id=1, source_target_pairs={{0,8},{1,9},{2,10},{3,11},{4,12},{5,13},{6,14},{7,15},{8,0},{9,1},... | collective-permute-start | bytes 20 | tf_op jit(solution)/shard_map/ppermute | solution.py:306
  47.4 3.1 %collective-permute-done.5 = f32[1]{0:T(128)} collective-permute-done((f32[1]{0:T(128)}, f32[1]{0:T(128)}, u32[]{:S(2)}, u32[]{:S(2)}) %collective-permute-start.5) | collective-permute-done | bytes 36 | tf_op jit(solution)/shard_map/ppermute | solution.py:306
  (1 shorter events, 0.0 us)
Async XLA Ops:
  0.6 3.6 %copy-start = (f32[3,16384]{1,0:T(4,128)S(1)}, f32[3,16384]{1,0:T(4,128)}, u32[]{:S(2)}) copy-start(f32[3,16384]{1,0:T(4,128)} %frac_ref.3) | copy-start | bytes 589828
  2.3 1.9 %copy-start.2 = (s32[16384]{0:T(1024)S(1)}, s32[16384]{0:T(1024)}, u32[]{:S(2)}) copy-start(s32[16384]{0:T(1024)} %param.9) | copy-start | bytes 196612
  4.2 1.0 %copy-start.1 = (f32[3,16384]{1,0:T(4,128)S(1)}, f32[3,16384]{1,0:T(4,128)}, u32[]{:S(2)}) copy-start(f32[3,16384]{1,0:T(4,128)} %vel_ref.3) | copy-start | bytes 589828
  5.2 0.8 %copy-start.3 = (f32[16384]{0:T(1024)S(1)}, f32[16384]{0:T(1024)}, u32[]{:S(2)}) copy-start(f32[16384]{0:T(1024)} %param.8) | copy-start | bytes 196612
  12.9 8.3 %collective-permute-start.1 = (f32[8,32,128]{2,1,0:T(8,128)S(1)}, f32[8,32,128]{2,1,0:T(8,128)S(1)}, u32[]{:S(2)}, u32[]{:S(2)}) collective-permute-start(f32[8,32,128]{2,1,0:T(8,128)S(1)} %get-tuple-element.8.low_ref), channel_id=1, source_target_pairs={{0,15},{1,0},{2,1},{3,2},{4,3},{5,4},{6,5},{7,6},{8,7},{9,8},{10,9... | collective-permute-start | bytes 393224 | tf_op jit(solution)/shard_map/ppermute | solution.py:38
  18.7 7.1 %collective-permute-start = (f32[8,32,128]{2,1,0:T(8,128)S(1)}, f32[8,32,128]{2,1,0:T(8,128)S(1)}, u32[]{:S(2)}, u32[]{:S(2)}) collective-permute-start(f32[8,32,128]{2,1,0:T(8,128)S(1)} %get-tuple-element.9.high_ref), channel_id=1, source_target_pairs={{0,1},{1,2},{2,3},{3,4},{4,5},{5,6},{6,7},{7,8},{8,9},{9,10},{10,1... | collective-permute-start | bytes 393224 | tf_op jit(solution)/shard_map/ppermute | solution.py:38
  35.0 1.2 %collective-permute-start.2 = (f32[1]{0:T(128)}, f32[1]{0:T(128)}, u32[]{:S(2)}, u32[]{:S(2)}) collective-permute-start(f32[1]{0:T(128)} %bitcast.5), channel_id=1, source_target_pairs={{0,1},{1,0},{2,3},{3,2},{4,5},{5,4},{6,7},{7,6},{8,9},{9,8},{10,11... | collective-permute-start | bytes 20 | tf_op jit(solution)/shard_map/ppermute | solution.py:306
  37.6 3.6 %collective-permute-start.3 = (f32[1]{0:T(128)}, f32[1]{0:T(128)}, u32[]{:S(2)}, u32[]{:S(2)}) collective-permute-start(f32[1]{0:T(128)} %max.12), channel_id=1, source_target_pairs={{0,2},{1,3},{2,0},{3,1},{4,6},{5,7},{6,4},{7,5},{8,10},{9,11},{10,... | collective-permute-start | bytes 20 | tf_op jit(solution)/shard_map/ppermute | solution.py:306
  41.8 3.6 %collective-permute-start.4 = (f32[1]{0:T(128)}, f32[1]{0:T(128)}, u32[]{:S(2)}, u32[]{:S(2)}) collective-permute-start(f32[1]{0:T(128)} %max.13), channel_id=1, source_target_pairs={{0,4},{1,5},{2,6},{3,7},{4,0},{5,1},{6,2},{7,3},{8,12},{9,13},{10,... | collective-permute-start | bytes 20 | tf_op jit(solution)/shard_map/ppermute | solution.py:306
  46.1 4.5 %collective-permute-start.5 = (f32[1]{0:T(128)}, f32[1]{0:T(128)}, u32[]{:S(2)}, u32[]{:S(2)}) collective-permute-start(f32[1]{0:T(128)} %max.14), channel_id=1, source_target_pairs={{0,8},{1,9},{2,10},{3,11},{4,12},{5,13},{6,14},{7,15},{8,0},{9,1},... | collective-permute-start | bytes 20 | tf_op jit(solution)/shard_map/ppermute | solution.py:306

commit v2 on v1

--- a/solution.py
+++ b/solution.py
@@ -292,20 +292,7 @@
 
     top = lax.fori_loop(0, blocks, finish, jnp.zeros((1, BLOCK), f32), unroll=4)
     top = jnp.sqrt(jnp.max(top, axis=1, keepdims=True))
-    top_ref[...] = jnp.broadcast_to(top, top_ref.shape)
-
-
-def largest(value, axis):
-    devices = lax.axis_size(axis)
-    reach = 1
-    while reach < devices:
-        if devices & (devices - 1) == 0:
-            pairs = [(i, i ^ reach) for i in range(devices)]
-        else:
-            pairs = [(i, (i + reach) % devices) for i in range(devices)]
-        value = jnp.maximum(value, lax.ppermute(value, axis, pairs))
-        reach *= 2
-    return value
+    top_ref[...] = jnp.broadcast_to(top[None], top_ref.shape)
 
 
 smem = pl.BlockSpec(memory_space=pltpu.SMEM)
@@ -339,7 +326,7 @@
         out_shape=(
             jax.ShapeDtypeStruct(frac.shape, f32),
             jax.ShapeDtypeStruct(velocity.shape, f32),
-            jax.ShapeDtypeStruct((8, 128), f32),
+            jax.ShapeDtypeStruct((lax.axis_size("gx"), 8, 128), f32),
         ),
         in_specs=[smem] * 5 + [vmem] * 7,
         out_specs=(vmem, vmem, vmem),
@@ -353,8 +340,8 @@
         tile_count, block, row, total, time_step,
         low, high, from_left, from_right, frac, velocity, cell_rows,
     )
-    fastest = largest(top[0, :1], "gx")
-    next_step = courant / (fastest + wave_speed)
+    tops = lax.all_to_all(top, "gx", 0, 0, tiled=True)
+    next_step = (courant / (jnp.max(tops) + wave_speed)).reshape(1)
     return (new_frac, new_velocity, next_step)
 
 

time: 51.9 us -> 45.1 us (0.87); the launches traced: 52.4 us -> 44.2 us
  blocking collectives: 0 us -> 9.47 us
  waiting for transfers between devices: 15.1 us -> 6.43 us
  starting transfers between devices: 9.91 us -> 4.25 us
  between operations: 6.63 us -> 3.85 us
  Pallas kernels: 15.6 us -> 14.9 us
  other arithmetic: 1.89 us -> 2.5 us
    all_to_all x0 -> x1, blocking collectives: none -> 9.47 us  [body(): tops = lax.all_to_all(top, 'gx', 0, 0, tiled=True)]
    ppermute x4 -> x0, waiting for transfers between devices: 8.7 us -> none  [largest(): value = jnp.maximum(value, lax.ppermute(value, axis, pairs))]
    ppermute x4 -> x0, starting transfers between devices: 4.11 us -> none  [largest(): value = jnp.maximum(value, lax.ppermute(value, axis, pairs))]
    ppermute x2, starting transfers between devices: 5.81 us -> 4.25 us  [shifted(): lax.ppermute(array, axis, [(i, (i + by) % devices) for i in range(devices)])]
    reduce_max x0 -> x1, other arithmetic: none -> 0.61 us  [body(): next_step = (courant / (jnp.max(tops) + wave_speed)).reshape(1)]
  transfers between devices with their start and end apart: 6 -> 2, of which waited for: 6 -> 2; matrix products, arithmetic and copies ran while one was open for 0% -> 0% of each run, Pallas kernels for 0% -> 0%
where the time goes in v2:
time: 45.1 us; the launch traced here: 44.2 us
  Pallas kernels  14.9 us (33%)
  blocking collectives  9.47 us (21%)
  waiting for transfers between devices  6.43 us (14%)
  starting transfers between devices  4.25 us (9%)
  between operations  3.85 us (9%)
  local copies, waits for them, and re-layouts  2.75 us (6%)
  other arithmetic  2.5 us (6%)
    all_to_all x1, blocking collectives, body(): tops = lax.all_to_all(top, 'gx', 0, 0, tiled=True)  9.47 us
    pallas_call x1, Pallas kernels, body(): pl.pallas_call(collect_kernel, out_shape=(jax.ShapeDtypeStruct(frac.shape...  8.33 us
    pallas_call x1, Pallas kernels, body(): pl.pallas_call(spread_kernel, out_shape=(layer_pair, layer_pair), in_spec...  6.6 us
    ppermute x2, waiting for transfers between devices, shifted(): lax.ppermute(array, axis, [(i, (i + by) % devices) for i in range(devices)])  6.43 us
    ppermute x2, starting transfers between devices, shifted(): lax.ppermute(array, axis, [(i, (i + by) % devices) for i in range(devices)])  4.25 us
    unnamed x8, local copies, waits for them, and re-layouts  1.79 us
  transfers between devices with their start and end apart: 2, of which 2 were waited for; matrix products, arithmetic and copies ran while one was open for 0% of the time, Pallas kernels for 0%

profile of v2, /device:TPU:0, one launch (start us, length us, event | category | flops | bytes accessed | tf_op | source)
XLA Modules:
  0.0 44.2 jit_solution(3304808099391458513)
XLA Ops:
  0.6 0.0 copy-start
  1.3 0.9 %reshape.159 = s32[64,256]{1,0:T(8,128)S(1)} reshape(s32[16384]{0:T(1024)} %param.9) | data formatting | bytes 131072 | tf_op jit(solution)/shard_map/reshape | solution.py:46
  2.2 0.1 select_reduce_fusion
  2.3 0.0 copy-start.2
  2.3 0.1 copy.17
  2.4 0.1 slice_reduce_fusion
  2.6 0.1 select_reduce_fusion.3
  2.7 0.7 %fusion.9 = (s32[]{:T(128)}, s32[64]{0:T(128)S(1)}, s32[64]{0:T(128)S(1)}) fusion(s32[64]{0:T(128)S(1)} %select_reduce_fusion, s32[]{:T(128)} %bitcast.8, s32[64]{0:T(128)S(1)} %get-tuple-element.13), kind=kLoop, calls=%fused_computation.39 | loop fusion | flops 2303 | bytes 1032 | tf_op jit(solution)/shard_map/reduce_sum | solution.py:53
  3.4 0.1 select_reduce_fusion.1
  3.5 0.7 %compare_select_fusion.row_ref = s32[128]{0:T(128)S(1)} fusion(s32[128]{0:T(128)S(1)} %get-tuple-element.15, s32[]{:T(128)} %get-tuple-element.17), kind=kLoop, calls=%fused_computation.29 | loop fusion | flops 384 | bytes 1028 | tf_op jit(solution)/shard_map/jit(_where)/select_n | solution.py:58
  4.2 0.0 copy-done
  4.2 0.0 copy-done.2
  4.2 0.0 copy-start.1
  4.2 0.9 %copy-done.1 = f32[3,16384]{1,0:T(4,128)S(1)} copy-done((f32[3,16384]{1,0:T(4,128)S(1)}, f32[3,16384]{1,0:T(4,128)}, u32[]{:S(2)}) %copy-start.1) | copy-done | bytes 196632
  5.2 0.0 copy-start.3
  5.2 0.8 %copy-done.3 = f32[16384]{0:T(1024)S(1)} copy-done((f32[16384]{0:T(1024)S(1)}, f32[16384]{0:T(1024)}, u32[]{:S(2)}) %copy-start.3) | copy-done | bytes 65560
  6.0 6.6 %spread.1 = (f32[8,32,128]{2,1,0:T(8,128)S(1)}, f32[8,32,128]{2,1,0:T(8,128)S(1)}) custom-call(s32[1]{0:T(128)} %copy.21.count_ref, s32[128]{0:T(128)S(1)} %get-tuple-element.16.block_ref, s32[128]{0:T(128)S(1)} %compare_select_fusion.row_ref, s32[1]{0:T(128)} %bitcast.2.total_ref, f32[3,16384]{1,0:T(4,128)S(1)} %copy-done, f32[3,16384]{1,0:T(4,128)S(1)} %copy-done.1, ...), custom_call_target="tpu_custom_call" | custom-call | tf_op jit(solution)/shard_map/spread/pallas_call | solution.py:310
  12.6 4.3 %collective-permute-start.1 = (f32[8,32,128]{2,1,0:T(8,128)S(1)}, f32[8,32,128]{2,1,0:T(8,128)S(1)}, u32[]{:S(2)}, u32[]{:S(2)}) collective-permute-start(f32[8,32,128]{2,1,0:T(8,128)S(1)} %get-tuple-element.8.low_ref), channel_id=1, source_target_pairs={{0,15},{1,0},{2,1},{3,2},{4,3},{5,4},{6,5},{7,6},{8,7},{9,8},{10,9... | collective-permute-start | bytes 393224 | tf_op jit(solution)/shard_map/ppermute | solution.py:38
  16.9 0.0 collective-permute-start
  17.5 1.9 %collective-permute-done.1.right_ref = f32[8,32,128]{2,1,0:T(8,128)S(1)} collective-permute-done((f32[8,32,128]{2,1,0:T(8,128)S(1)}, f32[8,32,128]{2,1,0:T(8,128)S(1)}, u32[]{:S(2)}, u32[]{:S(2)}) %collective-permute-start.1) | collective-permute-done | bytes 131104 | tf_op jit(solution)/shard_map/ppermute | solution.py:38
  19.4 4.6 %collective-permute-done.left_ref = f32[8,32,128]{2,1,0:T(8,128)S(1)} collective-permute-done((f32[8,32,128]{2,1,0:T(8,128)S(1)}, f32[8,32,128]{2,1,0:T(8,128)S(1)}, u32[]{:S(2)}, u32[]{:S(2)}) %collective-permute-start) | collective-permute-done | bytes 131104 | tf_op jit(solution)/shard_map/ppermute | solution.py:38
  24.0 8.3 %collect.1 = (f32[3,16384]{1,0:T(4,128)}, f32[3,16384]{1,0:T(4,128)}, f32[16,8,128]{2,1,0:T(8,128)S(1)}) custom-call(s32[1]{0:T(128)} %copy.21.count_ref, s32[128]{0:T(128)S(1)} %get-tuple-element.16.block_ref, s32[128]{0:T(128)S(1)} %compare_select_fusion.row_ref, s32[1]{0:T(128)} %bitcast.2.total_ref, f32[1]{0:T(128)S(6)} %copy.22.step_ref, ...), custom_call_target="tpu_custom_call" | custom-call | tf_op jit(solution)/shard_map/collect/pallas_call | solution.py:324
  32.3 9.5 %all_to_all.5 = f32[16,8,128]{2,1,0:T(8,128)S(1)} all-to-all(f32[16,8,128]{2,1,0:T(8,128)S(1)} %get-tuple-element.12), channel_id=1, replica_groups=mesh['runs'=2,'gx'=16] {'gx'}, dimensions={0} | all-to-all | bytes 131072 | tf_op jit(solution)/shard_map/all_to_all | solution.py:343
  41.8 0.6 %reduce_max.22 = f32[]{:T(128)} reduce(f32[16,8,128]{2,1,0:T(8,128)S(1)} %all_to_all.5, f32[]{:T(128)} %constant.36.clone.1), dimensions={0,1,2}, to_apply=%region_5.6 | reduce | flops 16383 | bytes 65544 | tf_op jit(solution)/shard_map/reduce_max | solution.py:344
  (1 shorter events, 0.0 us)
Async XLA Ops:
  0.6 3.6 %copy-start = (f32[3,16384]{1,0:T(4,128)S(1)}, f32[3,16384]{1,0:T(4,128)}, u32[]{:S(2)}) copy-start(f32[3,16384]{1,0:T(4,128)} %frac_ref.3) | copy-start | bytes 589828
  2.3 1.9 %copy-start.2 = (s32[16384]{0:T(1024)S(1)}, s32[16384]{0:T(1024)}, u32[]{:S(2)}) copy-start(s32[16384]{0:T(1024)} %param.9) | copy-start | bytes 196612
  4.2 1.0 %copy-start.1 = (f32[3,16384]{1,0:T(4,128)S(1)}, f32[3,16384]{1,0:T(4,128)}, u32[]{:S(2)}) copy-start(f32[3,16384]{1,0:T(4,128)} %vel_ref.3) | copy-start | bytes 589828
  5.2 0.8 %copy-start.3 = (f32[16384]{0:T(1024)S(1)}, f32[16384]{0:T(1024)}, u32[]{:S(2)}) copy-start(f32[16384]{0:T(1024)} %param.8) | copy-start | bytes 196612
  12.6 6.8 %collective-permute-start.1 = (f32[8,32,128]{2,1,0:T(8,128)S(1)}, f32[8,32,128]{2,1,0:T(8,128)S(1)}, u32[]{:S(2)}, u32[]{:S(2)}) collective-permute-start(f32[8,32,128]{2,1,0:T(8,128)S(1)} %get-tuple-element.8.low_ref), channel_id=1, source_target_pairs={{0,15},{1,0},{2,1},{3,2},{4,3},{5,4},{6,5},{7,6},{8,7},{9,8},{10,9... | collective-permute-start | bytes 393224 | tf_op jit(solution)/shard_map/ppermute | solution.py:38
  16.9 7.1 %collective-permute-start = (f32[8,32,128]{2,1,0:T(8,128)S(1)}, f32[8,32,128]{2,1,0:T(8,128)S(1)}, u32[]{:S(2)}, u32[]{:S(2)}) collective-permute-start(f32[8,32,128]{2,1,0:T(8,128)S(1)} %get-tuple-element.9.high_ref), channel_id=1, source_target_pairs={{0,1},{1,2},{2,3},{3,4},{4,5},{5,6},{6,7},{7,8},{8,9},{9,10},{10,1... | collective-permute-start | bytes 393224 | tf_op jit(solution)/shard_map/ppermute | solution.py:38

commit v3 on v1

--- a/solution.py
+++ b/solution.py
@@ -208,7 +208,7 @@
 def collect_kernel(
     count_ref, block_ref, row_ref, total_ref, step_ref,
     low_ref, high_ref, left_ref, right_ref, frac_ref, vel_ref, cells_ref,
-    new_frac_ref, new_vel_ref, top_ref, tab_ref, out_ref,
+    out_ref, top_ref, tab_ref,
 ):
     blocks = frac_ref.shape[1] // BLOCK
     count = count_ref[0]
@@ -284,15 +284,29 @@
         alive = at + lane < count
         got = out_ref[pl.ds(block, 1)][0]
         fresh = jnp.where(alive, flip_share * vel_ref[:, pl.ds(at, BLOCK)] + got[0:3], 0.0)
-        new_vel_ref[:, pl.ds(at, BLOCK)] = fresh
-        placed = jnp.where(alive, frac_ref[:, pl.ds(at, BLOCK)] + got[4:7], 0.0)
-        new_frac_ref[:, pl.ds(at, BLOCK)] = placed
+        out_ref[pl.ds(block, 1), 0:3] = fresh[None]
         square = fresh[0:1] * fresh[0:1] + fresh[1:2] * fresh[1:2] + fresh[2:3] * fresh[2:3]
         return jnp.maximum(top, square)
 
     top = lax.fori_loop(0, blocks, finish, jnp.zeros((1, BLOCK), f32), unroll=4)
     top = jnp.sqrt(jnp.max(top, axis=1, keepdims=True))
     top_ref[...] = jnp.broadcast_to(top, top_ref.shape)
+
+
+def finish_kernel(count_ref, moved_ref, frac_ref, new_frac_ref, new_vel_ref):
+    blocks = frac_ref.shape[1] // BLOCK
+    count = count_ref[0]
+    lane = lax.broadcasted_iota(jnp.int32, (1, BLOCK), 1)
+
+    def finish(block, carry):
+        at = pl.multiple_of(block * BLOCK, BLOCK)
+        got = moved_ref[pl.ds(block, 1)][0]
+        new_vel_ref[:, pl.ds(at, BLOCK)] = got[0:3]
+        placed = jnp.where(at + lane < count, frac_ref[:, pl.ds(at, BLOCK)] + got[4:7], 0.0)
+        new_frac_ref[:, pl.ds(at, BLOCK)] = placed
+        return carry
+
+    lax.fori_loop(0, blocks, finish, 0, unroll=4)
 
 
 def largest(value, axis):
@@ -334,27 +348,35 @@
     )(tile_count, block, row, total, frac, velocity, mass_rows, cell_rows)
     from_left = shifted(high, "gx", 1)
     from_right = shifted(low, "gx", -1)
-    new_frac, new_velocity, top = pl.pallas_call(
+    moved, top = pl.pallas_call(
         collect_kernel,
         out_shape=(
-            jax.ShapeDtypeStruct(frac.shape, f32),
-            jax.ShapeDtypeStruct(velocity.shape, f32),
+            jax.ShapeDtypeStruct((blocks, 8, BLOCK), f32),
             jax.ShapeDtypeStruct((8, 128), f32),
         ),
         in_specs=[smem] * 5 + [vmem] * 7,
-        out_specs=(vmem, vmem, vmem),
-        scratch_shapes=[
-            pltpu.VMEM((ROWS * TABLE, NZ), f32),
-            pltpu.VMEM((blocks, 8, BLOCK), f32),
-        ],
+        out_specs=(vmem, vmem),
+        scratch_shapes=[pltpu.VMEM((ROWS * TABLE, NZ), f32)],
         compiler_params=pltpu.CompilerParams(vmem_limit_bytes=32 * 1024 * 1024),
         name="collect",
     )(
         tile_count, block, row, total, time_step,
         low, high, from_left, from_right, frac, velocity, cell_rows,
     )
-    fastest = largest(top[0, :1], "gx")
-    next_step = courant / (fastest + wave_speed)
+    new_frac, new_velocity = pl.pallas_call(
+        finish_kernel,
+        out_shape=(
+            jax.ShapeDtypeStruct(frac.shape, f32),
+            jax.ShapeDtypeStruct(velocity.shape, f32),
+        ),
+        in_specs=[smem] + [vmem] * 2,
+        out_specs=(vmem, vmem),
+        compiler_params=pltpu.CompilerParams(vmem_limit_bytes=32 * 1024 * 1024),
+        cost_estimate=pl.CostEstimate(flops=0, bytes_accessed=8000000, transcendentals=0),
+        name="finish",
+    )(tile_count, moved, frac)
+    fastest = largest(top, "gx")
+    next_step = (courant / (fastest + wave_speed))[0, :1]
     return (new_frac, new_velocity, next_step)
 
 

time: 51.9 us -> 45 us (0.87); the launches traced: 52.4 us -> 44.4 us
  starting transfers between devices: 9.91 us -> 5.33 us
  between operations: 6.63 us -> 2.05 us
  waiting for transfers between devices: 15.1 us -> 18.2 us
  Pallas kernels: 15.6 us -> 13.8 us
    ppermute x4, starting transfers between devices: 4.11 us -> 0.15 us  [largest(): value = jnp.maximum(value, lax.ppermute(value, axis, pairs))]
    ppermute x4, waiting for transfers between devices: 8.7 us -> 11.7 us  [largest(): value = jnp.maximum(value, lax.ppermute(value, axis, pairs))]
    pallas_call x1, Pallas kernels: 6.92 us -> 5.94 us  [body(): pl.pallas_call(spread_kernel, out_shape=(layer_pair, layer_pair), in_spec...]
    pallas_call x1 -> x2, Pallas kernels: 8.64 us -> 7.89 us  [the longest x1 6.9 us: body(): pl.pallas_call(collect_kernel, out_shape=(jax.ShapeDtypeStruct((blocks, 8...]
    ppermute x2, starting transfers between devices: 5.81 us -> 5.18 us  [shifted(): lax.ppermute(array, axis, [(i, (i + by) % devices) for i in range(devices)])]
  transfers between devices with their start and end apart: 6 -> 6, of which waited for: 6 -> 6; matrix products, arithmetic and copies ran while one was open for 0% -> 0% of each run, Pallas kernels for 0% -> 2%
where the time goes in v3:
time: 45 us; the launch traced here: 44.4 us
  waiting for transfers between devices  18.2 us (40%)
  Pallas kernels  13.8 us (31%)
  starting transfers between devices  5.33 us (12%)
  local copies, waits for them, and re-layouts  3.27 us (7%)
  between operations  2.05 us (5%)
  other arithmetic  1.78 us (4%)
    ppermute x4, waiting for transfers between devices, largest(): value = jnp.maximum(value, lax.ppermute(value, axis, pairs))  11.7 us
    pallas_call x1, Pallas kernels, body(): pl.pallas_call(collect_kernel, out_shape=(jax.ShapeDtypeStruct((blocks, 8...  6.9 us
    ppermute x2, waiting for transfers between devices, shifted(): lax.ppermute(array, axis, [(i, (i + by) % devices) for i in range(devices)])  6.43 us
    pallas_call x1, Pallas kernels, body(): pl.pallas_call(spread_kernel, out_shape=(layer_pair, layer_pair), in_spec...  5.94 us
    ppermute x2, starting transfers between devices, shifted(): lax.ppermute(array, axis, [(i, (i + by) % devices) for i in range(devices)])  5.18 us
    unnamed x8, local copies, waits for them, and re-layouts  1.79 us
    pallas_call x1, Pallas kernels, body(): pl.pallas_call(finish_kernel, out_shape=(jax.ShapeDtypeStruct(frac.shape,...  1 us
  transfers between devices with their start and end apart: 6, of which 6 were waited for; matrix products, arithmetic and copies ran while one was open for 0% of the time, Pallas kernels for 2%

profile of v3, /device:TPU:0, one launch (start us, length us, event | category | flops | bytes accessed | tf_op | source)
XLA Modules:
  0.0 44.4 jit_solution(11072428084322836866)
XLA Ops:
  0.6 0.0 copy-start
  1.3 0.9 %reshape.156 = s32[64,256]{1,0:T(8,128)S(1)} reshape(s32[16384]{0:T(1024)} %param.9) | data formatting | bytes 131072 | tf_op jit(solution)/shard_map/reshape | solution.py:46
  2.2 0.1 select_reduce_fusion
  2.3 0.0 copy-start.2
  2.3 0.1 copy.17
  2.4 0.1 slice_reduce_fusion
  2.6 0.1 select_reduce_fusion.3
  2.7 0.6 %fusion.9 = (s32[]{:T(128)}, s32[64]{0:T(128)S(1)}, s32[64]{0:T(128)S(1)}) fusion(s32[64]{0:T(128)S(1)} %select_reduce_fusion, s32[]{:T(128)} %bitcast.8, s32[64]{0:T(128)S(1)} %get-tuple-element.15), kind=kLoop, calls=%fused_computation.40 | loop fusion | flops 2303 | bytes 1032 | tf_op jit(solution)/shard_map/reduce_sum | solution.py:53
  3.3 0.1 select_reduce_fusion.1
  3.4 0.7 %compare_select_fusion.row_ref = s32[128]{0:T(128)S(1)} fusion(s32[128]{0:T(128)S(1)} %get-tuple-element.17, s32[]{:T(128)} %get-tuple-element.19), kind=kLoop, calls=%fused_computation.30 | loop fusion | flops 384 | bytes 1028 | tf_op jit(solution)/shard_map/jit(_where)/select_n | solution.py:58
  4.1 0.0 copy-done
  4.1 0.0 copy-done.2
  4.1 0.0 copy-start.1
  4.1 0.9 %copy-done.1 = f32[3,16384]{1,0:T(4,128)S(1)} copy-done((f32[3,16384]{1,0:T(4,128)S(1)}, f32[3,16384]{1,0:T(4,128)}, u32[]{:S(2)}) %copy-start.1) | copy-done | bytes 196632
  5.1 0.0 copy-start.3
  5.1 0.8 %copy-done.3 = f32[16384]{0:T(1024)S(1)} copy-done((f32[16384]{0:T(1024)S(1)}, f32[16384]{0:T(1024)}, u32[]{:S(2)}) %copy-start.3) | copy-done | bytes 65560
  5.9 5.9 %spread.1 = (f32[8,32,128]{2,1,0:T(8,128)S(1)}, f32[8,32,128]{2,1,0:T(8,128)S(1)}) custom-call(s32[1]{0:T(128)} %copy.21.count_ref, s32[128]{0:T(128)S(1)} %get-tuple-element.18.block_ref, s32[128]{0:T(128)S(1)} %compare_select_fusion.row_ref, s32[1]{0:T(128)} %bitcast.2.total_ref, f32[3,16384]{1,0:T(4,128)S(1)} %copy-done, f32[3,16384]{1,0:T(4,128)S(1)} %copy-done.1, ...), custom_call_target="tpu_custom_call" | custom-call | tf_op jit(solution)/shard_map/spread/pallas_call | solution.py:337
  11.8 5.2 %collective-permute-start.1 = (f32[8,32,128]{2,1,0:T(8,128)S(1)}, f32[8,32,128]{2,1,0:T(8,128)S(1)}, u32[]{:S(2)}, u32[]{:S(2)}) collective-permute-start(f32[8,32,128]{2,1,0:T(8,128)S(1)} %get-tuple-element.9.low_ref), channel_id=1, source_target_pairs={{0,15},{1,0},{2,1},{3,2},{4,3},{5,4},{6,5},{7,6},{8,7},{9,8},{10,9... | collective-permute-start | bytes 393224 | tf_op jit(solution)/shard_map/ppermute | solution.py:38
  17.0 0.0 collective-permute-start
  17.7 1.9 %collective-permute-done.1.right_ref = f32[8,32,128]{2,1,0:T(8,128)S(1)} collective-permute-done((f32[8,32,128]{2,1,0:T(8,128)S(1)}, f32[8,32,128]{2,1,0:T(8,128)S(1)}, u32[]{:S(2)}, u32[]{:S(2)}) %collective-permute-start.1) | collective-permute-done | bytes 131104 | tf_op jit(solution)/shard_map/ppermute | solution.py:38
  19.5 4.6 %collective-permute-done.left_ref = f32[8,32,128]{2,1,0:T(8,128)S(1)} collective-permute-done((f32[8,32,128]{2,1,0:T(8,128)S(1)}, f32[8,32,128]{2,1,0:T(8,128)S(1)}, u32[]{:S(2)}, u32[]{:S(2)}) %collective-permute-start) | collective-permute-done | bytes 131104 | tf_op jit(solution)/shard_map/ppermute | solution.py:38
  24.1 6.9 %collect.1 = (f32[64,8,256]{2,1,0:T(8,128)S(1)}, f32[8,128]{1,0:T(8,128)S(1)}) custom-call(s32[1]{0:T(128)} %copy.21.count_ref, s32[128]{0:T(128)S(1)} %get-tuple-element.18.block_ref, s32[128]{0:T(128)S(1)} %compare_select_fusion.row_ref, s32[1]{0:T(128)} %bitcast.2.total_ref, f32[1]{0:T(128)S(6)} %copy.22.step_ref, ...), custom_call_target="tpu_custom_call" | custom-call | tf_op jit(solution)/shard_map/collect/pallas_call | solution.py:351
  31.0 0.0 collective-permute-start.2
  31.0 1.2 %collective-permute-done.2 = f32[8,128]{1,0:T(8,128)S(1)} collective-permute-done((f32[8,128]{1,0:T(8,128)S(1)}, f32[8,128]{1,0:T(8,128)S(1)}, u32[]{:S(2)}, u32[]{:S(2)}) %collective-permute-start.2) | collective-permute-done | bytes 4128 | tf_op jit(solution)/shard_map/ppermute | solution.py:320
  32.2 0.0 collective-permute-start.3
  32.2 3.6 %collective-permute-done.3 = f32[8,128]{1,0:T(8,128)S(1)} collective-permute-done((f32[8,128]{1,0:T(8,128)S(1)}, f32[8,128]{1,0:T(8,128)S(1)}, u32[]{:S(2)}, u32[]{:S(2)}) %collective-permute-start.3) | collective-permute-done | bytes 4128 | tf_op jit(solution)/shard_map/ppermute | solution.py:320
  35.8 0.0 collective-permute-start.4
  35.8 3.6 %collective-permute-done.4 = f32[8,128]{1,0:T(8,128)S(1)} collective-permute-done((f32[8,128]{1,0:T(8,128)S(1)}, f32[8,128]{1,0:T(8,128)S(1)}, u32[]{:S(2)}, u32[]{:S(2)}) %collective-permute-start.4) | collective-permute-done | bytes 4128 | tf_op jit(solution)/shard_map/ppermute | solution.py:320
  39.4 0.1 collective-permute-start.5
  39.5 1.0 %finish.1 = (f32[3,16384]{1,0:T(4,128)}, f32[3,16384]{1,0:T(4,128)}) custom-call(s32[1]{0:T(128)} %copy.21.count_ref, f32[64,8,256]{2,1,0:T(8,128)S(1)} %get-tuple-element.11.moved_ref, f32[3,16384]{1,0:T(4,128)S(1)} %copy-done), custom_call_target="tpu_custom_call" | custom-call | bytes 8000000 | tf_op jit(solution)/shard_map/finish/pallas_call | solution.py:366
  40.5 3.4 %collective-permute-done.5 = f32[8,128]{1,0:T(8,128)S(1)} collective-permute-done((f32[8,128]{1,0:T(8,128)S(1)}, f32[8,128]{1,0:T(8,128)S(1)}, u32[]{:S(2)}, u32[]{:S(2)}) %collective-permute-start.5) | collective-permute-done | bytes 4128 | tf_op jit(solution)/shard_map/ppermute | solution.py:320
  43.9 0.5 %slice.7 = f32[1,1]{1,0:T(1,128)} slice(f32[8,128]{1,0:T(8,128)S(1)} %add_divide_fusion), slice={[0:1], [0:1]} | slice | bytes 8 | tf_op jit(solution)/shard_map/slice | solution.py:379
  (5 shorter events, 0.0 us)
Async XLA Ops:
  0.6 3.5 %copy-start = (f32[3,16384]{1,0:T(4,128)S(1)}, f32[3,16384]{1,0:T(4,128)}, u32[]{:S(2)}) copy-start(f32[3,16384]{1,0:T(4,128)} %frac_ref.5) | copy-start | bytes 589828
  2.3 1.8 %copy-start.2 = (s32[16384]{0:T(1024)S(1)}, s32[16384]{0:T(1024)}, u32[]{:S(2)}) copy-start(s32[16384]{0:T(1024)} %param.9) | copy-start | bytes 196612
  4.1 1.0 %copy-start.1 = (f32[3,16384]{1,0:T(4,128)S(1)}, f32[3,16384]{1,0:T(4,128)}, u32[]{:S(2)}) copy-start(f32[3,16384]{1,0:T(4,128)} %vel_ref.3) | copy-start | bytes 589828
  5.1 0.8 %copy-start.3 = (f32[16384]{0:T(1024)S(1)}, f32[16384]{0:T(1024)}, u32[]{:S(2)}) copy-start(f32[16384]{0:T(1024)} %param.8) | copy-start | bytes 196612
  11.8 7.7 %collective-permute-start.1 = (f32[8,32,128]{2,1,0:T(8,128)S(1)}, f32[8,32,128]{2,1,0:T(8,128)S(1)}, u32[]{:S(2)}, u32[]{:S(2)}) collective-permute-start(f32[8,32,128]{2,1,0:T(8,128)S(1)} %get-tuple-element.9.low_ref), channel_id=1, source_target_pairs={{0,15},{1,0},{2,1},{3,2},{4,3},{5,4},{6,5},{7,6},{8,7},{9,8},{10,9... | collective-permute-start | bytes 393224 | tf_op jit(solution)/shard_map/ppermute | solution.py:38
  17.0 7.1 %collective-permute-start = (f32[8,32,128]{2,1,0:T(8,128)S(1)}, f32[8,32,128]{2,1,0:T(8,128)S(1)}, u32[]{:S(2)}, u32[]{:S(2)}) collective-permute-start(f32[8,32,128]{2,1,0:T(8,128)S(1)} %get-tuple-element.10.high_ref), channel_id=1, source_target_pairs={{0,1},{1,2},{2,3},{3,4},{4,5},{5,6},{6,7},{7,8},{8,9},{9,10},{10,1... | collective-permute-start | bytes 393224 | tf_op jit(solution)/shard_map/ppermute | solution.py:38
  31.0 1.2 %collective-permute-start.2 = (f32[8,128]{1,0:T(8,128)S(1)}, f32[8,128]{1,0:T(8,128)S(1)}, u32[]{:S(2)}, u32[]{:S(2)}) collective-permute-start(f32[8,128]{1,0:T(8,128)S(1)} %get-tuple-element.14), channel_id=1, source_target_pairs={{0,1},{1,0},{2,3},{3,2},{4,5},{5,4},{6,7},{7,6},{8,9},{9,8},{10,11... | collective-permute-start | bytes 12296 | tf_op jit(solution)/shard_map/ppermute | solution.py:320
  32.2 3.6 %collective-permute-start.3 = (f32[8,128]{1,0:T(8,128)S(1)}, f32[8,128]{1,0:T(8,128)S(1)}, u32[]{:S(2)}, u32[]{:S(2)}) collective-permute-start(f32[8,128]{1,0:T(8,128)S(1)} %max.12), channel_id=1, source_target_pairs={{0,2},{1,3},{2,0},{3,1},{4,6},{5,7},{6,4},{7,5},{8,10},{9,11},{10,... | collective-permute-start | bytes 12296 | tf_op jit(solution)/shard_map/ppermute | solution.py:320
  35.8 3.6 %collective-permute-start.4 = (f32[8,128]{1,0:T(8,128)S(1)}, f32[8,128]{1,0:T(8,128)S(1)}, u32[]{:S(2)}, u32[]{:S(2)}) collective-permute-start(f32[8,128]{1,0:T(8,128)S(1)} %max.13), channel_id=1, source_target_pairs={{0,4},{1,5},{2,6},{3,7},{4,0},{5,1},{6,2},{7,3},{8,12},{9,13},{10,... | collective-permute-start | bytes 12296 | tf_op jit(solution)/shard_map/ppermute | solution.py:320
  39.4 4.5 %collective-permute-start.5 = (f32[8,128]{1,0:T(8,128)S(1)}, f32[8,128]{1,0:T(8,128)S(1)}, u32[]{:S(2)}, u32[]{:S(2)}) collective-permute-start(f32[8,128]{1,0:T(8,128)S(1)} %max.14), channel_id=1, source_target_pairs={{0,8},{1,9},{2,10},{3,11},{4,12},{5,13},{6,14},{7,15},{8,0},{9,1},... | collective-permute-start | bytes 12296 | tf_op jit(solution)/shard_map/ppermute | solution.py:320

commit v4 on v3

--- a/solution.py
+++ b/solution.py
@@ -311,14 +311,17 @@
 
 def largest(value, axis):
     devices = lax.axis_size(axis)
-    reach = 1
+    reach, radix = 1, 2
     while reach < devices:
+        ahead = [k * reach for k in range(1, radix) if k * reach < devices]
         if devices & (devices - 1) == 0:
-            pairs = [(i, i ^ reach) for i in range(devices)]
+            pairs = [[(i, i ^ by) for i in range(devices)] for by in ahead]
         else:
-            pairs = [(i, (i + reach) % devices) for i in range(devices)]
-        value = jnp.maximum(value, lax.ppermute(value, axis, pairs))
-        reach *= 2
+            pairs = [[(i, (i + by) % devices) for i in range(devices)] for by in ahead]
+        arrived = [lax.ppermute(value, axis, listed) for listed in pairs]
+        for other in arrived:
+            value = jnp.maximum(value, other)
+        reach, radix = reach * radix, 8
     return value
 
 

time: 45 us -> 46.2 us (1.027)
  the two profiles are of different devices: /device:TPU:0 before, /device:TPU:6 now
where the time goes in v4:
time: 46.2 us; the launch traced here: 45.5 us
  starting transfers between devices  17.1 us (37%)
  Pallas kernels  12.6 us (27%)
  waiting for transfers between devices  8.66 us (19%)
  local copies, waits for them, and re-layouts  3.27 us (7%)
  between operations  2.06 us (4%)
  other arithmetic  1.78 us (4%)
    ppermute x8, starting transfers between devices, largest(): arrived = [lax.ppermute(value, axis, listed) for listed in pairs]  16.5 us
    pallas_call x1, Pallas kernels, body(): pl.pallas_call(collect_kernel, out_shape=(jax.ShapeDtypeStruct((blocks, 8...  6.29 us
    pallas_call x1, Pallas kernels, body(): pl.pallas_call(spread_kernel, out_shape=(layer_pair, layer_pair), in_spec...  5.31 us
    ppermute x2, waiting for transfers between devices, shifted(): lax.ppermute(array, axis, [(i, (i + by) % devices) for i in range(devices)])  4.89 us
    ppermute x8, waiting for transfers between devices, largest(): arrived = [lax.ppermute(value, axis, listed) for listed in pairs]  3.77 us
    unnamed x8, local copies, waits for them, and re-layouts  1.79 us
    pallas_call x1, Pallas kernels, body(): pl.pallas_call(finish_kernel, out_shape=(jax.ShapeDtypeStruct(frac.shape,...  1 us
  transfers between devices with their start and end apart: 10, of which 5 were waited for; matrix products, arithmetic and copies ran while one was open for 0% of the time, Pallas kernels for 2%

profile of v4, /device:TPU:6, one launch (start us, length us, event | category | flops | bytes accessed | tf_op | source)
XLA Modules:
  0.0 45.5 jit_solution(18306905133233981432)
XLA Ops:
  0.6 0.0 copy-start
  1.3 0.9 %reshape.156 = s32[64,256]{1,0:T(8,128)S(1)} reshape(s32[16384]{0:T(1024)} %param.9) | data formatting | bytes 131072 | tf_op jit(solution)/shard_map/reshape | solution.py:46
  2.2 0.1 select_reduce_fusion
  2.3 0.0 copy-start.2
  2.3 0.1 copy.17
  2.4 0.1 slice_reduce_fusion
  2.6 0.1 select_reduce_fusion.3
  2.7 0.6 %fusion.9 = (s32[]{:T(128)}, s32[64]{0:T(128)S(1)}, s32[64]{0:T(128)S(1)}) fusion(s32[64]{0:T(128)S(1)} %select_reduce_fusion, s32[]{:T(128)} %bitcast.8, s32[64]{0:T(128)S(1)} %get-tuple-element.15), kind=kLoop, calls=%fused_computation.40 | loop fusion | flops 2303 | bytes 1032 | tf_op jit(solution)/shard_map/reduce_sum | solution.py:53
  3.3 0.1 select_reduce_fusion.1
  3.4 0.7 %compare_select_fusion.row_ref = s32[128]{0:T(128)S(1)} fusion(s32[128]{0:T(128)S(1)} %get-tuple-element.17, s32[]{:T(128)} %get-tuple-element.19), kind=kLoop, calls=%fused_computation.30 | loop fusion | flops 384 | bytes 1028 | tf_op jit(solution)/shard_map/jit(_where)/select_n | solution.py:58
  4.1 0.0 copy-done
  4.1 0.0 copy-done.2
  4.1 0.0 copy-start.1
  4.1 0.9 %copy-done.1 = f32[3,16384]{1,0:T(4,128)S(1)} copy-done((f32[3,16384]{1,0:T(4,128)S(1)}, f32[3,16384]{1,0:T(4,128)}, u32[]{:S(2)}) %copy-start.1) | copy-done | bytes 196632
  5.1 0.0 copy-start.3
  5.1 0.8 %copy-done.3 = f32[16384]{0:T(1024)S(1)} copy-done((f32[16384]{0:T(1024)S(1)}, f32[16384]{0:T(1024)}, u32[]{:S(2)}) %copy-start.3) | copy-done | bytes 65560
  5.9 5.3 %spread.1 = (f32[8,32,128]{2,1,0:T(8,128)S(1)}, f32[8,32,128]{2,1,0:T(8,128)S(1)}) custom-call(s32[1]{0:T(128)} %copy.21.count_ref, s32[128]{0:T(128)S(1)} %get-tuple-element.18.block_ref, s32[128]{0:T(128)S(1)} %compare_select_fusion.row_ref, s32[1]{0:T(128)} %bitcast.2.total_ref, f32[3,16384]{1,0:T(4,128)S(1)} %copy-done, f32[3,16384]{1,0:T(4,128)S(1)} %copy-done.1, ...), custom_call_target="tpu_custom_call" | custom-call | tf_op jit(solution)/shard_map/spread/pallas_call | solution.py:340
  11.2 0.3 collective-permute-start.1
  11.5 0.3 collective-permute-start
  12.4 1.6 %collective-permute-done.1.right_ref = f32[8,32,128]{2,1,0:T(8,128)S(1)} collective-permute-done((f32[8,32,128]{2,1,0:T(8,128)S(1)}, f32[8,32,128]{2,1,0:T(8,128)S(1)}, u32[]{:S(2)}, u32[]{:S(2)}) %collective-permute-start.1) | collective-permute-done | bytes 131104 | tf_op jit(solution)/shard_map/ppermute | solution.py:38
  14.0 3.3 %collective-permute-done.left_ref = f32[8,32,128]{2,1,0:T(8,128)S(1)} collective-permute-done((f32[8,32,128]{2,1,0:T(8,128)S(1)}, f32[8,32,128]{2,1,0:T(8,128)S(1)}, u32[]{:S(2)}, u32[]{:S(2)}) %collective-permute-start) | collective-permute-done | bytes 131104 | tf_op jit(solution)/shard_map/ppermute | solution.py:38
  17.3 6.3 %collect.1 = (f32[64,8,256]{2,1,0:T(8,128)S(1)}, f32[8,128]{1,0:T(8,128)S(1)}) custom-call(s32[1]{0:T(128)} %copy.21.count_ref, s32[128]{0:T(128)S(1)} %get-tuple-element.18.block_ref, s32[128]{0:T(128)S(1)} %compare_select_fusion.row_ref, s32[1]{0:T(128)} %bitcast.2.total_ref, f32[1]{0:T(128)S(6)} %copy.22.step_ref, ...), custom_call_target="tpu_custom_call" | custom-call | tf_op jit(solution)/shard_map/collect/pallas_call | solution.py:354
  23.6 0.0 collective-permute-start.2
  23.6 1.2 %collective-permute-done.2 = f32[8,128]{1,0:T(8,128)S(1)} collective-permute-done((f32[8,128]{1,0:T(8,128)S(1)}, f32[8,128]{1,0:T(8,128)S(1)}, u32[]{:S(2)}, u32[]{:S(2)}) %collective-permute-start.2) | collective-permute-done | bytes 4128 | tf_op jit(solution)/shard_map/ppermute | solution.py:321
  24.8 6.7 %collective-permute-start.9 = (f32[8,128]{1,0:T(8,128)S(1)}, f32[8,128]{1,0:T(8,128)S(1)}, u32[]{:S(2)}, u32[]{:S(2)}) collective-permute-start(f32[8,128]{1,0:T(8,128)S(1)} %max.24), channel_id=1, source_target_pairs={{0,14},{1,15},{2,12},{3,13},{4,10},{5,11},{6,8},{7,9},{8,6},{9,7},... | collective-permute-start | bytes 12296 | tf_op jit(solution)/shard_map/ppermute | solution.py:321
  31.5 3.9 %collective-permute-start.8 = (f32[8,128]{1,0:T(8,128)S(1)}, f32[8,128]{1,0:T(8,128)S(1)}, u32[]{:S(2)}, u32[]{:S(2)}) collective-permute-start(f32[8,128]{1,0:T(8,128)S(1)} %max.24), channel_id=1, source_target_pairs={{0,12},{1,13},{2,14},{3,15},{4,8},{5,9},{6,10},{7,11},{8,4},{9,5},... | collective-permute-start | bytes 12296 | tf_op jit(solution)/shard_map/ppermute | solution.py:321
  35.5 0.0 collective-permute-start.7
  35.5 0.4 collective-permute-start.6
  35.9 1.5 %collective-permute-start.5 = (f32[8,128]{1,0:T(8,128)S(1)}, f32[8,128]{1,0:T(8,128)S(1)}, u32[]{:S(2)}, u32[]{:S(2)}) collective-permute-start(f32[8,128]{1,0:T(8,128)S(1)} %max.24), channel_id=1, source_target_pairs={{0,6},{1,7},{2,4},{3,5},{4,2},{5,3},{6,0},{7,1},{8,14},{9,15},{10,... | collective-permute-start | bytes 12296 | tf_op jit(solution)/shard_map/ppermute | solution.py:321
  37.3 0.0 collective-permute-done.9
  37.3 4.0 %collective-permute-start.4 = (f32[8,128]{1,0:T(8,128)S(1)}, f32[8,128]{1,0:T(8,128)S(1)}, u32[]{:S(2)}, u32[]{:S(2)}) collective-permute-start(f32[8,128]{1,0:T(8,128)S(1)} %max.24), channel_id=1, source_target_pairs={{0,4},{1,5},{2,6},{3,7},{4,0},{5,1},{6,2},{7,3},{8,12},{9,13},{10,... | collective-permute-start | bytes 12296 | tf_op jit(solution)/shard_map/ppermute | solution.py:321
  41.3 0.0 collective-permute-done.8
  41.3 0.0 collective-permute-start.3
  41.3 1.0 %finish.1 = (f32[3,16384]{1,0:T(4,128)}, f32[3,16384]{1,0:T(4,128)}) custom-call(s32[1]{0:T(128)} %copy.21.count_ref, f32[64,8,256]{2,1,0:T(8,128)S(1)} %get-tuple-element.11.moved_ref, f32[3,16384]{1,0:T(4,128)S(1)} %copy-done), custom_call_target="tpu_custom_call" | custom-call | bytes 8000000 | tf_op jit(solution)/shard_map/finish/pallas_call | solution.py:369
  42.3 0.0 collective-permute-done.7
  42.3 0.0 collective-permute-done.6
  42.3 0.0 collective-permute-done.5
  42.3 0.6 %collective-permute-done.4 = f32[8,128]{1,0:T(8,128)S(1)} collective-permute-done((f32[8,128]{1,0:T(8,128)S(1)}, f32[8,128]{1,0:T(8,128)S(1)}, u32[]{:S(2)}, u32[]{:S(2)}) %collective-permute-start.4) | collective-permute-done | bytes 4128 | tf_op jit(solution)/shard_map/ppermute | solution.py:321
  42.9 2.0 %collective-permute-done.3 = f32[8,128]{1,0:T(8,128)S(1)} collective-permute-done((f32[8,128]{1,0:T(8,128)S(1)}, f32[8,128]{1,0:T(8,128)S(1)}, u32[]{:S(2)}, u32[]{:S(2)}) %collective-permute-start.3) | collective-permute-done | bytes 4128 | tf_op jit(solution)/shard_map/ppermute | solution.py:321
  44.9 0.5 %slice.7 = f32[1,1]{1,0:T(1,128)} slice(f32[8,128]{1,0:T(8,128)S(1)} %add_divide_fusion), slice={[0:1], [0:1]} | slice | bytes 8 | tf_op jit(solution)/shard_map/slice | solution.py:382
  (3 shorter events, 0.0 us)
Async XLA Ops:
  0.6 3.5 %copy-start = (f32[3,16384]{1,0:T(4,128)S(1)}, f32[3,16384]{1,0:T(4,128)}, u32[]{:S(2)}) copy-start(f32[3,16384]{1,0:T(4,128)} %frac_ref.5) | copy-start | bytes 589828
  2.3 1.8 %copy-start.2 = (s32[16384]{0:T(1024)S(1)}, s32[16384]{0:T(1024)}, u32[]{:S(2)}) copy-start(s32[16384]{0:T(1024)} %param.9) | copy-start | bytes 196612
  4.1 1.0 %copy-start.1 = (f32[3,16384]{1,0:T(4,128)S(1)}, f32[3,16384]{1,0:T(4,128)}, u32[]{:S(2)}) copy-start(f32[3,16384]{1,0:T(4,128)} %vel_ref.3) | copy-start | bytes 589828
  5.1 0.8 %copy-start.3 = (f32[16384]{0:T(1024)S(1)}, f32[16384]{0:T(1024)}, u32[]{:S(2)}) copy-start(f32[16384]{0:T(1024)} %param.8) | copy-start | bytes 196612
  11.2 2.8 %collective-permute-start.1 = (f32[8,32,128]{2,1,0:T(8,128)S(1)}, f32[8,32,128]{2,1,0:T(8,128)S(1)}, u32[]{:S(2)}, u32[]{:S(2)}) collective-permute-start(f32[8,32,128]{2,1,0:T(8,128)S(1)} %get-tuple-element.9.low_ref), channel_id=1, source_target_pairs={{0,15},{1,0},{2,1},{3,2},{4,3},{5,4},{6,5},{7,6},{8,7},{9,8},{10,9... | collective-permute-start | bytes 393224 | tf_op jit(solution)/shard_map/ppermute | solution.py:38
  11.5 5.8 %collective-permute-start = (f32[8,32,128]{2,1,0:T(8,128)S(1)}, f32[8,32,128]{2,1,0:T(8,128)S(1)}, u32[]{:S(2)}, u32[]{:S(2)}) collective-permute-start(f32[8,32,128]{2,1,0:T(8,128)S(1)} %get-tuple-element.10.high_ref), channel_id=1, source_target_pairs={{0,1},{1,2},{2,3},{3,4},{4,5},{5,6},{6,7},{7,8},{8,9},{9,10},{10,1... | collective-permute-start | bytes 393224 | tf_op jit(solution)/shard_map/ppermute | solution.py:38
  23.6 1.2 %collective-permute-start.2 = (f32[8,128]{1,0:T(8,128)S(1)}, f32[8,128]{1,0:T(8,128)S(1)}, u32[]{:S(2)}, u32[]{:S(2)}) collective-permute-start(f32[8,128]{1,0:T(8,128)S(1)} %get-tuple-element.14), channel_id=1, source_target_pairs={{0,1},{1,0},{2,3},{3,2},{4,5},{5,4},{6,7},{7,6},{8,9},{9,8},{10,11... | collective-permute-start | bytes 12296 | tf_op jit(solution)/shard_map/ppermute | solution.py:321
  24.8 12.5 %collective-permute-start.9 = (f32[8,128]{1,0:T(8,128)S(1)}, f32[8,128]{1,0:T(8,128)S(1)}, u32[]{:S(2)}, u32[]{:S(2)}) collective-permute-start(f32[8,128]{1,0:T(8,128)S(1)} %max.24), channel_id=1, source_target_pairs={{0,14},{1,15},{2,12},{3,13},{4,10},{5,11},{6,8},{7,9},{8,6},{9,7},... | collective-permute-start | bytes 12296 | tf_op jit(solution)/shard_map/ppermute | solution.py:321
  31.5 9.8 %collective-permute-start.8 = (f32[8,128]{1,0:T(8,128)S(1)}, f32[8,128]{1,0:T(8,128)S(1)}, u32[]{:S(2)}, u32[]{:S(2)}) collective-permute-start(f32[8,128]{1,0:T(8,128)S(1)} %max.24), channel_id=1, source_target_pairs={{0,12},{1,13},{2,14},{3,15},{4,8},{5,9},{6,10},{7,11},{8,4},{9,5},... | collective-permute-start | bytes 12296 | tf_op jit(solution)/shard_map/ppermute | solution.py:321
  35.5 6.9 %collective-permute-start.7 = (f32[8,128]{1,0:T(8,128)S(1)}, f32[8,128]{1,0:T(8,128)S(1)}, u32[]{:S(2)}, u32[]{:S(2)}) collective-permute-start(f32[8,128]{1,0:T(8,128)S(1)} %max.24), channel_id=1, source_target_pairs={{0,10},{1,11},{2,8},{3,9},{4,14},{5,15},{6,12},{7,13},{8,2},{9,3},... | collective-permute-start | bytes 12296 | tf_op jit(solution)/shard_map/ppermute | solution.py:321
  35.5 6.9 %collective-permute-start.6 = (f32[8,128]{1,0:T(8,128)S(1)}, f32[8,128]{1,0:T(8,128)S(1)}, u32[]{:S(2)}, u32[]{:S(2)}) collective-permute-start(f32[8,128]{1,0:T(8,128)S(1)} %max.24), channel_id=1, source_target_pairs={{0,8},{1,9},{2,10},{3,11},{4,12},{5,13},{6,14},{7,15},{8,0},{9,1},... | collective-permute-start | bytes 12296 | tf_op jit(solution)/shard_map/ppermute | solution.py:321
  35.9 6.5 %collective-permute-start.5 = (f32[8,128]{1,0:T(8,128)S(1)}, f32[8,128]{1,0:T(8,128)S(1)}, u32[]{:S(2)}, u32[]{:S(2)}) collective-permute-start(f32[8,128]{1,0:T(8,128)S(1)} %max.24), channel_id=1, source_target_pairs={{0,6},{1,7},{2,4},{3,5},{4,2},{5,3},{6,0},{7,1},{8,14},{9,15},{10,... | collective-permute-start | bytes 12296 | tf_op jit(solution)/shard_map/ppermute | solution.py:321
  37.3 5.6 %collective-permute-start.4 = (f32[8,128]{1,0:T(8,128)S(1)}, f32[8,128]{1,0:T(8,128)S(1)}, u32[]{:S(2)}, u32[]{:S(2)}) collective-permute-start(f32[8,128]{1,0:T(8,128)S(1)} %max.24), channel_id=1, source_target_pairs={{0,4},{1,5},{2,6},{3,7},{4,0},{5,1},{6,2},{7,3},{8,12},{9,13},{10,... | collective-permute-start | bytes 12296 | tf_op jit(solution)/shard_map/ppermute | solution.py:321
  41.3 3.6 %collective-permute-start.3 = (f32[8,128]{1,0:T(8,128)S(1)}, f32[8,128]{1,0:T(8,128)S(1)}, u32[]{:S(2)}, u32[]{:S(2)}) collective-permute-start(f32[8,128]{1,0:T(8,128)S(1)} %max.24), channel_id=1, source_target_pairs={{0,2},{1,3},{2,0},{3,1},{4,6},{5,7},{6,4},{7,5},{8,10},{9,11},{10,... | collective-permute-start | bytes 12296 | tf_op jit(solution)/shard_map/ppermute | solution.py:321

commit v5 on v3

v5 whole, which is shorter than its diff:
```python
import functools

import jax
import jax.numpy as jnp
from jax import lax
from jax.experimental import pallas as pl
from jax.experimental.pallas import tpu as pltpu
from jax.sharding import PartitionSpec as P

CX = 2
NY = 32
NZ = 128
ROWS = CX * NY
BLOCK = 256
LANES = 128
UNROLL = 8
SPREAD = 32
TABLE = 16

mass_floor = 0.25
stiffness = 2.0
press_floor = 1.0
grain_size = 0.5
inertia_ref = 0.3
mu_static = 0.38
mu_limit = 0.64
rate_floor = 0.5
gravity = (0.5, 0.0, -0.866)
flip_share = 0.95
courant = 0.4
wave_speed = 2.0
components = ((0, 3, 4), (3, 1, 5), (4, 5, 2))
f32 = jnp.float32
bf16 = jnp.bfloat16


def shifted(array, axis, by):
    devices = lax.axis_size(axis)
    return lax.ppermute(array, axis, [(i, (i + by) % devices) for i in range(devices)])


def split_pair(values):
    high = values.astype(bf16)
    low = (values - high.astype(f32)).astype(bf16)
    return high, low


def one_hot(cells_ref, block, offset):
    rel = cells_ref[pl.ds(block * 2, 2), :] - offset
    nodes = lax.broadcasted_iota(jnp.int32, (NZ, LANES), 0)
    halves = [jnp.where(nodes == rel[h : h + 1, :], 1.0, 0.0) for h in range(2)]
    return jnp.concatenate(halves, axis=1).astype(bf16)


def spread_kernel(
    count_hbm, frac_hbm, vel_hbm, mass_hbm, cells_hbm,
    low_ref, high_ref, plan_ref,
    count_ref, listed_ref, frac_ref, vel_ref, mass_ref, cells_ref, q_ref, acc_ref, sems,
):
    slots = frac_ref.shape[1]
    blocks = slots // BLOCK
    steps = blocks + ROWS
    arrivals = [
        pltpu.make_async_copy(source, target, sems.at[k])
        for k, (source, target) in enumerate(
            (
                (count_hbm, count_ref),
                (cells_hbm, listed_ref),
                (frac_hbm, frac_ref),
                (vel_hbm, vel_ref),
                (mass_hbm, mass_ref),
                (cells_hbm, cells_ref),
            )
        )
    ]
    for arrival in arrivals:
        arrival.start()
    acc_ref[...] = jnp.zeros_like(acc_ref)
    for arrival in arrivals:
        arrival.wait()
    count = count_ref[0]
    live_blocks = (count + BLOCK - 1) >> 8
    sublane = lax.broadcasted_iota(jnp.int32, (8, LANES), 0)
    lane = lax.broadcasted_iota(jnp.int32, (1, LANES), 1)
    top_z = sublane >= 4
    field = sublane & 3

    def list_visit(v, block, row, total):
        valid = block < live_blocks
        plan_ref[v] = jnp.where(valid, block, 0)
        plan_ref[steps + v] = jnp.where(valid, row + (row >> 5), 0)
        plan_ref[2 * steps + v] = jnp.where(valid, row, ROWS) * NZ
        end = jnp.minimum(block * BLOCK + BLOCK, count) - 1
        after = jnp.minimum(block * BLOCK + BLOCK, slots - 1)
        last = listed_ref[end >> 7, end & 127] >> 7
        following = listed_ref[after >> 7, after & 127] >> 7
        ahead = valid & (row >= last)
        return (
            jnp.where(ahead, block + 1, block),
            jnp.where(ahead, following, row + 1),
            jnp.where(valid, v + 1, total),
        )

    def weigh(part):
        at = pl.multiple_of(part * LANES, LANES)
        here = pl.ds(at, LANES)

        def spread_out(line):
            return jnp.broadcast_to(line, (8, LANES))

        fx, fy, fz = (spread_out(frac_ref[d : d + 1, here]) for d in range(3))
        vx, vy, vz = (spread_out(vel_ref[d : d + 1, here]) for d in range(3))
        held = spread_out(jnp.where(at + lane < count, mass_ref[pl.ds(part, 1), :], 0.0))
        carried = jnp.where(
            field == 0, held, held * jnp.where(field == 1, vx, jnp.where(field == 2, vy, vz))
        )
        carried = carried * jnp.where(top_z, fz, 1.0 - fz)
        lower, upper = carried * (1.0 - fx), carried * fx
        rows = jnp.concatenate(
            [lower * (1.0 - fy), lower * fy, upper * (1.0 - fy), upper * fy], axis=0
        )
        high, low = split_pair(rows)
        q_ref[pl.ds(part, 1)] = jnp.concatenate([high, low], axis=0)[None]

    def prepare(group, carry):
        block, row, total = carry
        for u in range(UNROLL):
            v = group * UNROLL + u
            block, row, total = list_visit(v, block, row, total)
            weigh(v)
        return block, row, total

    start = (jnp.int32(0), listed_ref[0, 0] >> 7, jnp.int32(0))
    total = lax.fori_loop(0, steps // UNROLL, prepare, start)[2]
    plan_ref[3 * steps] = total
    plan_ref[3 * steps + 1] = count

    def visit(group, carry):
        found = []
        for u in range(UNROLL):
            v = group * UNROLL + u
            block = plan_ref[v]
            hot = one_hot(cells_ref, block, plan_ref[2 * steps + v])
            both = q_ref[pl.ds(block * 2, 2)]
            both = lax.dot_general(
                jnp.concatenate([both[0], both[1]], axis=1),
                hot,
                (((1,), (1,)), ((), ())),
                preferred_element_type=f32,
            )
            found.append((plan_ref[steps + v], both[:SPREAD] + both[SPREAD:]))
        for base, part in found:
            for k, ahead in enumerate((0, 1, NY + 1, NY + 2)):
                at = pl.ds(pl.multiple_of((base + ahead) * 8, 8), 8)
                acc_ref[at, :] += part[8 * k : 8 * k + 8]
        return carry

    lax.fori_loop(0, (total + UNROLL - 1) // UNROLL, visit, 0)

    for l in range(CX + 1):
        first = l * (NY + 1) * 8
        acc_ref[first : first + 8, :] += acc_ref[first + NY * 8 : first + NY * 8 + 8, :]
        for f in range(4):
            lower = acc_ref[pl.ds(first + f, NY, stride=8), :]
            upper = acc_ref[pl.ds(first + 4 + f, NY, stride=8), :]
            summed = lower + pltpu.roll(upper, 1, 1)
            if l < CX:
                low_ref[f * CX + l] = summed
            if l > 0:
                high_ref[f * CX + l - 1] = summed


def pair_up(field, axis):
    return field + pltpu.roll(field, field.shape[axis] - 1, axis)


def step_up(field, axis):
    return pltpu.roll(field, field.shape[axis] - 1, axis) - field


def pair_down(field, axis):
    return field + pltpu.roll(field, 1, axis)


def step_down(field, axis):
    return field - pltpu.roll(field, 1, axis)


def cell_stress(vel_lo, vel_hi, mass_lo, mass_hi, keep):
    grads = []
    for a in range(3):
        diff = vel_hi[a] - vel_lo[a]
        both = vel_hi[a] + vel_lo[a]
        grads.append(
            [
                0.25 * pair_up(pair_up(diff, 0), 1),
                0.25 * pair_up(step_up(both, 0), 1),
                0.25 * step_up(pair_up(both, 0), 1),
            ]
        )
    density = 0.125 * pair_up(pair_up(mass_hi + mass_lo, 0), 1)
    dxx = grads[0][0]
    dyy = grads[1][1]
    dzz = grads[2][2]
    dxy = 0.5 * (grads[0][1] + grads[1][0])
    dxz = 0.5 * (grads[0][2] + grads[2][0])
    dyz = 0.5 * (grads[1][2] + grads[2][1])
    second = dxx * dxx + dyy * dyy + dzz * dzz + 2.0 * (dxy * dxy + dxz * dxz + dyz * dyz)
    rate = jnp.sqrt(2.0 * second + rate_floor * rate_floor)
    pressure = stiffness * density
    inertial = rate * grain_size / jnp.sqrt(pressure + press_floor)
    friction = mu_static + (mu_limit - mu_static) * inertial / (inertia_ref + inertial)
    twice = 2.0 * friction * pressure / rate
    sigma = [
        twice * dxx - pressure,
        twice * dyy - pressure,
        twice * dzz - pressure,
        twice * dxy,
        twice * dxz,
        twice * dyz,
    ]
    return [jnp.where(keep, s, 0.0) for s in sigma]


def node_force(lower, upper):
    force = []
    for a in range(3):
        sx, sy, sz = (components[a][b] for b in range(3))
        along = pair_down(pair_down(upper[sx] - lower[sx], 0), 1)
        across = step_down(pair_down(upper[sy] + lower[sy], 1), 0)
        upward = step_down(pair_down(upper[sz] + lower[sz], 0), 1)
        force.append(0.25 * (along + across + upward))
    return force


def collect_kernel(
    plan_ref, step_ref, low_ref, high_ref, left_ref, right_ref, frac_ref, vel_ref, cells_ref,
    out_ref, top_ref, tab_ref, pair_ref,
):
    blocks = frac_ref.shape[1] // BLOCK
    steps = blocks + ROWS
    total = plan_ref[3 * steps]
    count = plan_ref[3 * steps + 1]
    step = step_ref[0]
    nodes = [
        [left_ref[f * 2] for f in range(4)],
        [low_ref[f * 2] + left_ref[f * 2 + 1] for f in range(4)],
        [low_ref[f * 2 + 1] for f in range(4)],
        [high_ref[f * 2 + 1] + right_ref[f * 2] for f in range(4)],
        [right_ref[f * 2 + 1] for f in range(4)],
    ]
    height = lax.broadcasted_iota(jnp.int32, (NY, NZ), 1)
    keep = height < NZ - 1
    above_bed = height > 0
    floor = [jnp.maximum(layer[0], mass_floor) for layer in nodes]
    v_old = [[layer[1 + a] / floor[l] for a in range(3)] for l, layer in enumerate(nodes)]
    sigma = [
        cell_stress(v_old[l], v_old[l + 1], nodes[l][0], nodes[l + 1][0], keep) for l in range(4)
    ]
    blank = jnp.zeros((NY, NZ), f32)
    for l in range(CX + 1):
        force = node_force(sigma[l], sigma[l + 1])
        fields = [blank] * 8
        for a in range(3):
            layer = nodes[l + 1]
            fresh = (layer[1 + a] + step * (force[a] + layer[0] * gravity[a])) / floor[l + 1]
            fresh = jnp.where(above_bed, fresh, 0.0)
            fields[a] = fresh - flip_share * v_old[l + 1][a]
            fields[4 + a] = step * fresh
        for k, value in enumerate(fields):
            start = l * NY * TABLE + k
            tab_ref[pl.ds(start, NY, stride=TABLE), :] = value
            tab_ref[pl.ds(start + 8, NY, stride=TABLE), :] = pltpu.roll(value, NZ - 1, 1)

    for l in range(CX + 1):

        def split_row(j, carry):
            at = pl.ds(pl.multiple_of((l * NY + j) * TABLE, TABLE), TABLE)
            high, low = split_pair(tab_ref[at, :])
            pair_ref[pl.ds(l * (NY + 1) + j, 1)] = jnp.concatenate([high, low], axis=0)[None]
            return carry

        lax.fori_loop(0, NY, split_row, 0, unroll=8)
        pair_ref[l * (NY + 1) + NY] = pair_ref[l * (NY + 1)]

    out_ref[...] = jnp.zeros_like(out_ref)

    def visit(group, carry):
        found = []
        for u in range(UNROLL):
            v = group * UNROLL + u
            block = plan_ref[v]
            base = plan_ref[steps + v]
            hot = one_hot(cells_ref, block, plan_ref[2 * steps + v])
            rows = [pair_ref[base + ahead] for ahead in (0, 1, NY + 1, NY + 2)]
            both = jnp.dot(jnp.concatenate(rows, axis=0), hot, preferred_element_type=f32)
            corners = []
            for k in range(4):
                four = both[4 * 8 * k : 4 * 8 * (k + 1)]
                corners += [four[0:8] + four[16:24], four[8:16] + four[24:32]]
            frac = frac_ref[:, pl.ds(pl.multiple_of(block * BLOCK, BLOCK), BLOCK)]
            for d in (2, 1, 0):
                share = frac[d : d + 1, :]
                corners = [
                    corners[k] + share * (corners[k + 1] - corners[k])
                    for k in range(0, len(corners), 2)
                ]
            found.append((block, corners[0]))
        for block, part in found:
            out_ref[pl.ds(block, 1)] += part[None]
        return carry

    lax.fori_loop(0, (total + UNROLL - 1) // UNROLL, visit, 0)

    lane = lax.broadcasted_iota(jnp.int32, (1, BLOCK), 1)

    def finish(block, top):
        at = pl.multiple_of(block * BLOCK, BLOCK)
        alive = at + lane < count
        got = out_ref[pl.ds(block, 1)][0]
        fresh = jnp.where(alive, flip_share * vel_ref[:, pl.ds(at, BLOCK)] + got[0:3], 0.0)
        out_ref[pl.ds(block, 1), 0:3] = fresh[None]
        square = fresh[0:1] * fresh[0:1] + fresh[1:2] * fresh[1:2] + fresh[2:3] * fresh[2:3]
        return jnp.maximum(top, square)

    top = lax.fori_loop(0, blocks, finish, jnp.zeros((1, BLOCK), f32), unroll=4)
    top = jnp.sqrt(jnp.max(top, axis=1, keepdims=True))
    top_ref[...] = jnp.broadcast_to(top, top_ref.shape)


def finish_kernel(plan_ref, moved_ref, frac_ref, new_frac_ref, new_vel_ref):
    blocks = frac_ref.shape[1] // BLOCK
    count = plan_ref[3 * (blocks + ROWS) + 1]
    lane = lax.broadcasted_iota(jnp.int32, (1, BLOCK), 1)

    def finish(block, carry):
        at = pl.multiple_of(block * BLOCK, BLOCK)
        got = moved_ref[pl.ds(block, 1)][0]
        new_vel_ref[:, pl.ds(at, BLOCK)] = got[0:3]
        placed = jnp.where(at + lane < count, frac_ref[:, pl.ds(at, BLOCK)] + got[4:7], 0.0)
        new_frac_ref[:, pl.ds(at, BLOCK)] = placed
        return carry

    lax.fori_loop(0, blocks, finish, 0, unroll=4)


def largest(value, axis):
    devices = lax.axis_size(axis)
    reach = 1
    while reach < devices:
        if devices & (devices - 1) == 0:
            pairs = [(i, i ^ reach) for i in range(devices)]
        else:
            pairs = [(i, (i + reach) % devices) for i in range(devices)]
        value = jnp.maximum(value, lax.ppermute(value, axis, pairs))
        reach *= 2
    return value


smem = pl.BlockSpec(memory_space=pltpu.SMEM)
vmem = pl.BlockSpec(memory_space=pltpu.VMEM)
hbm = pl.BlockSpec(memory_space=pltpu.HBM)


def body(frac, velocity, mass, particle_cell, tile_count, time_step):
    slots = frac.shape[1]
    blocks = slots // BLOCK
    steps = blocks + ROWS
    mass_rows = mass.reshape(slots // LANES, LANES)
    cell_rows = particle_cell.reshape(slots // LANES, LANES)
    layer_pair = jax.ShapeDtypeStruct((4 * CX, NY, NZ), f32)
    low, high, plan = pl.pallas_call(
        spread_kernel,
        out_shape=(layer_pair, layer_pair, jax.ShapeDtypeStruct((4 * steps,), jnp.int32)),
        in_specs=[hbm] * 5,
        out_specs=(vmem, vmem, smem),
        scratch_shapes=[
            pltpu.SMEM((1,), jnp.int32),
            pltpu.SMEM((slots // LANES, LANES), jnp.int32),
            pltpu.VMEM((3, slots), f32),
            pltpu.VMEM((3, slots), f32),
            pltpu.VMEM((slots // LANES, LANES), f32),
            pltpu.VMEM((slots // LANES, LANES), jnp.int32),
            pltpu.VMEM((slots // LANES, 2 * SPREAD, LANES), bf16),
            pltpu.VMEM(((CX + 1) * (NY + 1) * 8, NZ), f32),
            pltpu.SemaphoreType.DMA((6,)),
        ],
        compiler_params=pltpu.CompilerParams(vmem_limit_bytes=32 * 1024 * 1024),
        name="spread",
    )(tile_count, frac, velocity, mass_rows, cell_rows)
    from_left = shifted(high, "gx", 1)
    from_right = shifted(low, "gx", -1)
    moved, top = pl.pallas_call(
        collect_kernel,
        out_shape=(
            jax.ShapeDtypeStruct((blocks, 8, BLOCK), f32),
            jax.ShapeDtypeStruct((8, LANES), f32),
        ),
        in_specs=[smem] * 2 + [vmem] * 7,
        out_specs=(vmem, vmem),
        scratch_shapes=[
            pltpu.VMEM(((CX + 1) * NY * TABLE, NZ), f32),
            pltpu.VMEM(((CX + 1) * (NY + 1), 2 * TABLE, NZ), bf16),
        ],
        compiler_params=pltpu.CompilerParams(vmem_limit_bytes=32 * 1024 * 1024),
        name="collect",
    )(plan, time_step, low, high, from_left, from_right, frac, velocity, cell_rows)
    new_frac, new_velocity = pl.pallas_call(
        finish_kernel,
        out_shape=(
            jax.ShapeDtypeStruct(frac.shape, f32),
            jax.ShapeDtypeStruct(velocity.shape, f32),
        ),
        in_specs=[smem] + [vmem] * 2,
        out_specs=(vmem, vmem),
        compiler_params=pltpu.CompilerParams(vmem_limit_bytes=32 * 1024 * 1024),
        cost_estimate=pl.CostEstimate(flops=0, bytes_accessed=8000000, transcendentals=0),
        name="finish",
    )(plan, moved, frac)
    fastest = largest(top, "gx")
    next_step = (courant / (fastest + wave_speed))[0, :1]
    return (new_frac, new_velocity, next_step)


def solution(mesh):
    placed = (
        P(None, ("runs", "gx")),
        P(None, ("runs", "gx")),
        P(("runs", "gx")),
        P(("runs", "gx")),
        P(("runs", "gx")),
        P("runs"),
    )
    return jax.shard_map(
        body,
        mesh=mesh,
        in_specs=placed,
        out_specs=(P(None, ("runs", "gx")), P(None, ("runs", "gx")), P("runs")),
        check_vma=False,
    )
```

time: 45 us -> 44.4 us (0.987)
  other arithmetic: 1.78 us -> 0.02 us
  Pallas kernels: 13.8 us -> 15.1 us
  local copies, waits for them, and re-layouts: 3.27 us -> 4.09 us
  waiting for transfers between devices: 18.2 us -> 17.6 us
    pallas_call x1, Pallas kernels: 5.94 us -> 7.79 us  [body(): pl.pallas_call(spread_kernel, out_shape=(layer_pair, layer_pair, jax.Shap...]
    unnamed x8 -> x10, local copies, waits for them, and re-layouts: 1.79 us -> 3.57 us
    pallas_call x1, Pallas kernels: 6.9 us -> 5.75 us  [body(): pl.pallas_call(collect_kernel, out_shape=(jax.ShapeDtypeStruct((blocks, 8...]
    reshape x1 -> x0, local copies, waits for them, and re-layouts: 0.86 us -> none  [visit_list(): cells = particle_cell.reshape(blocks, BLOCK)]
    reduce_sum x3 -> x0, other arithmetic: 0.85 us -> none  [the longest x1 0.64 us: visit_list(): total = jnp.sum(visits)]
    select_n x1 -> x0, other arithmetic: 0.65 us -> none  [visit_list(): row = jnp.where(order < total, row, ROWS)]
    pallas_call x1, Pallas kernels: 1 us -> 1.56 us  [body(): pl.pallas_call(finish_kernel, out_shape=(jax.ShapeDtypeStruct(frac.shape,...]
    ppermute x4, waiting for transfers between devices: 11.7 us -> 11.2 us  [largest(): value = jnp.maximum(value, lax.ppermute(value, axis, pairs))]
  transfers between devices with their start and end apart: 6 -> 6, of which waited for: 6 -> 6; matrix products, arithmetic and copies ran while one was open for 0% -> 0% of each run, Pallas kernels for 2% -> 4%
where the time goes in v5:
time: 44.4 us; the launch traced here: 44.1 us
  waiting for transfers between devices  17.6 us (40%)
  Pallas kernels  15.1 us (34%)
  starting transfers between devices  5.32 us (12%)
  local copies, waits for them, and re-layouts  4.09 us (9%)
  between operations  1.97 us (4%)
    ppermute x4, waiting for transfers between devices, largest(): value = jnp.maximum(value, lax.ppermute(value, axis, pairs))  11.2 us
    pallas_call x1, Pallas kernels, body(): pl.pallas_call(spread_kernel, out_shape=(layer_pair, layer_pair, jax.Shap...  7.79 us
    ppermute x2, waiting for transfers between devices, shifted(): lax.ppermute(array, axis, [(i, (i + by) % devices) for i in range(devices)])  6.43 us
    pallas_call x1, Pallas kernels, body(): pl.pallas_call(collect_kernel, out_shape=(jax.ShapeDtypeStruct((blocks, 8...  5.75 us
    ppermute x2, starting transfers between devices, shifted(): lax.ppermute(array, axis, [(i, (i + by) % devices) for i in range(devices)])  5.18 us
    unnamed x10, local copies, waits for them, and re-layouts  3.57 us
    pallas_call x1, Pallas kernels, body(): pl.pallas_call(finish_kernel, out_shape=(jax.ShapeDtypeStruct(frac.shape,...  1.56 us
  transfers between devices with their start and end apart: 6, of which 6 were waited for; matrix products, arithmetic and copies ran while one was open for 0% of the time, Pallas kernels for 4%

profile of v5, /device:TPU:0, one launch (start us, length us, event | category | flops | bytes accessed | tf_op | source)
XLA Modules:
  0.0 44.1 jit_solution(5950434063089714649)
XLA Ops:
  1.3 0.0 copy-start
  1.3 0.9 %copy-done = f32[3,16384]{1,0:T(4,128)S(1)} copy-done((f32[3,16384]{1,0:T(4,128)S(1)}, f32[3,16384]{1,0:T(4,128)}, u32[]{:S(2)}) %copy-start) | copy-done | bytes 196632
  2.2 0.0 copy-start.1
  2.2 0.9 %copy-done.1 = f32[3,16384]{1,0:T(4,128)S(1)} copy-done((f32[3,16384]{1,0:T(4,128)S(1)}, f32[3,16384]{1,0:T(4,128)}, u32[]{:S(2)}) %copy-start.1) | copy-done | bytes 196632
  3.2 0.0 copy-start.2
  3.2 0.8 %copy-done.2 = s32[16384]{0:T(1024)S(1)} copy-done((s32[16384]{0:T(1024)S(1)}, s32[16384]{0:T(1024)}, u32[]{:S(2)}) %copy-start.2) | copy-done | bytes 65560
  4.0 0.0 copy-start.4
  4.0 0.8 %copy-done.4 = f32[16384]{0:T(1024)S(1)} copy-done((f32[16384]{0:T(1024)S(1)}, f32[16384]{0:T(1024)}, u32[]{:S(2)}) %copy-start.4) | copy-done | bytes 65560
  4.9 0.0 copy-start.3
  4.9 7.8 %spread.1 = (f32[8,32,128]{2,1,0:T(8,128)S(1)}, f32[8,32,128]{2,1,0:T(8,128)S(1)}, s32[512]{0:T(512)S(1)}) custom-call(s32[1]{0:T(128)S(6)} %copy.9.count_hbm, f32[3,16384]{1,0:T(4,128)S(1)} %copy-done, f32[3,16384]{1,0:T(4,128)S(1)} %copy-done.1, f32[128,128]{1,0:T(8,128)S(1)} %bitcast.5, s32[128,128]{1,0:T(8,128)S(1)} %bitcast.3), custom_call_target="tpu_custom_call" | custom-call | tf_op jit(solution)/shard_map/spread/pallas_call | solution.py:372
  12.7 5.2 %collective-permute-start.1 = (f32[8,32,128]{2,1,0:T(8,128)S(1)}, f32[8,32,128]{2,1,0:T(8,128)S(1)}, u32[]{:S(2)}, u32[]{:S(2)}) collective-permute-start(f32[8,32,128]{2,1,0:T(8,128)S(1)} %get-tuple-element.11.low_ref), channel_id=1, source_target_pairs={{0,15},{1,0},{2,1},{3,2},{4,3},{5,4},{6,5},{7,6},{8,7},{9,8},{10,9... | collective-permute-start | bytes 393224 | tf_op jit(solution)/shard_map/ppermute | solution.py:39
  17.8 0.0 collective-permute-start
  18.5 1.9 %collective-permute-done.1.right_ref = f32[8,32,128]{2,1,0:T(8,128)S(1)} collective-permute-done((f32[8,32,128]{2,1,0:T(8,128)S(1)}, f32[8,32,128]{2,1,0:T(8,128)S(1)}, u32[]{:S(2)}, u32[]{:S(2)}) %collective-permute-start.1) | collective-permute-done | bytes 131104 | tf_op jit(solution)/shard_map/ppermute | solution.py:39
  20.4 4.6 %collective-permute-done.left_ref = f32[8,32,128]{2,1,0:T(8,128)S(1)} collective-permute-done((f32[8,32,128]{2,1,0:T(8,128)S(1)}, f32[8,32,128]{2,1,0:T(8,128)S(1)}, u32[]{:S(2)}, u32[]{:S(2)}) %collective-permute-start) | collective-permute-done | bytes 131104 | tf_op jit(solution)/shard_map/ppermute | solution.py:39
  24.9 0.0 copy-done.3
  24.9 5.7 %collect.1 = (f32[64,8,256]{2,1,0:T(8,128)S(1)}, f32[8,128]{1,0:T(8,128)S(1)}) custom-call(s32[512]{0:T(512)S(1)} %get-tuple-element.10.plan_ref, f32[1]{0:T(128)S(6)} %copy.10.step_ref, f32[8,32,128]{2,1,0:T(8,128)S(1)} %get-tuple-element.11.low_ref, f32[8,32,128]{2,1,0:T(8,128)S(1)} %get-tuple-element.12.high_ref, ...), custom_call_target="tpu_custom_call" | custom-call | tf_op jit(solution)/shard_map/collect/pallas_call | solution.py:393
  30.7 0.0 collective-permute-start.2
  30.7 1.2 %collective-permute-done.2 = f32[8,128]{1,0:T(8,128)S(1)} collective-permute-done((f32[8,128]{1,0:T(8,128)S(1)}, f32[8,128]{1,0:T(8,128)S(1)}, u32[]{:S(2)}, u32[]{:S(2)}) %collective-permute-start.2) | collective-permute-done | bytes 4128 | tf_op jit(solution)/shard_map/ppermute | solution.py:355
  31.9 0.0 collective-permute-start.3
  31.9 3.6 %collective-permute-done.3 = f32[8,128]{1,0:T(8,128)S(1)} collective-permute-done((f32[8,128]{1,0:T(8,128)S(1)}, f32[8,128]{1,0:T(8,128)S(1)}, u32[]{:S(2)}, u32[]{:S(2)}) %collective-permute-start.3) | collective-permute-done | bytes 4128 | tf_op jit(solution)/shard_map/ppermute | solution.py:355
  35.5 0.0 collective-permute-start.4
  35.5 3.6 %collective-permute-done.4 = f32[8,128]{1,0:T(8,128)S(1)} collective-permute-done((f32[8,128]{1,0:T(8,128)S(1)}, f32[8,128]{1,0:T(8,128)S(1)}, u32[]{:S(2)}, u32[]{:S(2)}) %collective-permute-start.4) | collective-permute-done | bytes 4128 | tf_op jit(solution)/shard_map/ppermute | solution.py:355
  39.1 0.1 collective-permute-start.5
  39.2 1.6 %finish.1 = (f32[3,16384]{1,0:T(4,128)}, f32[3,16384]{1,0:T(4,128)}) custom-call(s32[512]{0:T(512)S(1)} %get-tuple-element.10.plan_ref, f32[64,8,256]{2,1,0:T(8,128)S(1)} %get-tuple-element.13.moved_ref, f32[3,16384]{1,0:T(4,128)S(1)} %copy-done), custom_call_target="tpu_custom_call" | custom-call | bytes 8000000 | tf_op jit(solution)/shard_map/finish/pallas_call | solution.py:408
  40.8 2.8 %collective-permute-done.5 = f32[8,128]{1,0:T(8,128)S(1)} collective-permute-done((f32[8,128]{1,0:T(8,128)S(1)}, f32[8,128]{1,0:T(8,128)S(1)}, u32[]{:S(2)}, u32[]{:S(2)}) %collective-permute-start.5) | collective-permute-done | bytes 4128 | tf_op jit(solution)/shard_map/ppermute | solution.py:355
  43.6 0.5 %slice.3 = f32[1,1]{1,0:T(1,128)} slice(f32[8,128]{1,0:T(8,128)S(1)} %add_divide_fusion), slice={[0:1], [0:1]} | slice | bytes 8 | tf_op jit(solution)/shard_map/slice | solution.py:421
  (4 shorter events, 0.0 us)
Async XLA Ops:
  1.3 1.0 %copy-start = (f32[3,16384]{1,0:T(4,128)S(1)}, f32[3,16384]{1,0:T(4,128)}, u32[]{:S(2)}) copy-start(f32[3,16384]{1,0:T(4,128)} %frac_ref.3) | copy-start | bytes 589828
  2.2 0.9 %copy-start.1 = (f32[3,16384]{1,0:T(4,128)S(1)}, f32[3,16384]{1,0:T(4,128)}, u32[]{:S(2)}) copy-start(f32[3,16384]{1,0:T(4,128)} %vel_ref.1) | copy-start | bytes 589828
  3.2 0.8 %copy-start.2 = (s32[16384]{0:T(1024)S(1)}, s32[16384]{0:T(1024)}, u32[]{:S(2)}) copy-start(s32[16384]{0:T(1024)} %param.9) | copy-start | bytes 196612
  4.0 0.8 %copy-start.4 = (f32[16384]{0:T(1024)S(1)}, f32[16384]{0:T(1024)}, u32[]{:S(2)}) copy-start(f32[16384]{0:T(1024)} %param.8) | copy-start | bytes 196612
  4.9 20.1 %copy-start.3 = (s32[16384]{0:T(1024)S(1)}, s32[16384]{0:T(1024)}, u32[]{:S(2)}) copy-start(s32[16384]{0:T(1024)} %param.9) | copy-start | bytes 196612
  12.7 7.7 %collective-permute-start.1 = (f32[8,32,128]{2,1,0:T(8,128)S(1)}, f32[8,32,128]{2,1,0:T(8,128)S(1)}, u32[]{:S(2)}, u32[]{:S(2)}) collective-permute-start(f32[8,32,128]{2,1,0:T(8,128)S(1)} %get-tuple-element.11.low_ref), channel_id=1, source_target_pairs={{0,15},{1,0},{2,1},{3,2},{4,3},{5,4},{6,5},{7,6},{8,7},{9,8},{10,9... | collective-permute-start | bytes 393224 | tf_op jit(solution)/shard_map/ppermute | solution.py:39
  17.8 7.1 %collective-permute-start = (f32[8,32,128]{2,1,0:T(8,128)S(1)}, f32[8,32,128]{2,1,0:T(8,128)S(1)}, u32[]{:S(2)}, u32[]{:S(2)}) collective-permute-start(f32[8,32,128]{2,1,0:T(8,128)S(1)} %get-tuple-element.12.high_ref), channel_id=1, source_target_pairs={{0,1},{1,2},{2,3},{3,4},{4,5},{5,6},{6,7},{7,8},{8,9},{9,10},{10,1... | collective-permute-start | bytes 393224 | tf_op jit(solution)/shard_map/ppermute | solution.py:39
  30.7 1.2 %collective-permute-start.2 = (f32[8,128]{1,0:T(8,128)S(1)}, f32[8,128]{1,0:T(8,128)S(1)}, u32[]{:S(2)}, u32[]{:S(2)}) collective-permute-start(f32[8,128]{1,0:T(8,128)S(1)} %get-tuple-element.16), channel_id=1, source_target_pairs={{0,1},{1,0},{2,3},{3,2},{4,5},{5,4},{6,7},{7,6},{8,9},{9,8},{10,11... | collective-permute-start | bytes 12296 | tf_op jit(solution)/shard_map/ppermute | solution.py:355
  31.9 3.6 %collective-permute-start.3 = (f32[8,128]{1,0:T(8,128)S(1)}, f32[8,128]{1,0:T(8,128)S(1)}, u32[]{:S(2)}, u32[]{:S(2)}) collective-permute-start(f32[8,128]{1,0:T(8,128)S(1)} %max.12), channel_id=1, source_target_pairs={{0,2},{1,3},{2,0},{3,1},{4,6},{5,7},{6,4},{7,5},{8,10},{9,11},{10,... | collective-permute-start | bytes 12296 | tf_op jit(solution)/shard_map/ppermute | solution.py:355
  35.5 3.6 %collective-permute-start.4 = (f32[8,128]{1,0:T(8,128)S(1)}, f32[8,128]{1,0:T(8,128)S(1)}, u32[]{:S(2)}, u32[]{:S(2)}) collective-permute-start(f32[8,128]{1,0:T(8,128)S(1)} %max.13), channel_id=1, source_target_pairs={{0,4},{1,5},{2,6},{3,7},{4,0},{5,1},{6,2},{7,3},{8,12},{9,13},{10,... | collective-permute-start | bytes 12296 | tf_op jit(solution)/shard_map/ppermute | solution.py:355
  39.1 4.5 %collective-permute-start.5 = (f32[8,128]{1,0:T(8,128)S(1)}, f32[8,128]{1,0:T(8,128)S(1)}, u32[]{:S(2)}, u32[]{:S(2)}) collective-permute-start(f32[8,128]{1,0:T(8,128)S(1)} %max.14), channel_id=1, source_target_pairs={{0,8},{1,9},{2,10},{3,11},{4,12},{5,13},{6,14},{7,15},{8,0},{9,1},... | collective-permute-start | bytes 12296 | tf_op jit(solution)/shard_map/ppermute | solution.py:355
